TPU v7x, 512 devices: a whole 4x8x8 slice. The times are simulated.
512 devices in a mesh: sector: 32 (over x, y), op: 16 (over z, core).
Axes of the slice: x: 4, y: 8, z: 8, core: 2. Of those that a mesh axis runs over, the one named last changes fastest.
Arguments:
- wavefunction: bfloat16 [2, 256, 128, 128], P(None, 'sector'), may hold values from -6 to 6
- right_blocks: bfloat16 [256, 128, 128, 128], P('sector', 'op'), may hold values from -0.5 to 0.5
- left_blocks: bfloat16 [256, 128, 128, 128], P('sector', 'op'), may hold values from -0.0625 to 0.0625
- targets: int32 [256, 128], P('sector', 'op'), may hold values from 0 to 255, as said below
Outputs:
- sigma_blocks: float32 [2, 256, 128, 128], P(None, 'sector', 'op')
Inputs may be any that keep to these rules, and one draw needn't show every extreme that they name: Sector t is owned by index t // 8 of sector. Among the pairs of one device (8 source sectors times the 8 terms of one op index) at most 4 have targets on any one owner; in every draw one owner receives exactly 4 from every device.
All inputs are finite; a program needn't handle non-finite values.
Results may differ from a plain program's by a relative error of at most 0.0037.
Values may be sent and summed in bfloat16 or wider, within the bound.
No kernel may reach another device: no remote copies, remote signals or barrier semaphores. Data moves between devices by JAX's collectives and lax.ppermute only.
A program may use at most 64 MiB of HBM per device.

v0:
```python
import jax
import jax.numpy as jnp
from jax import lax
from jax.sharding import PartitionSpec as P


def right_products(vectors, right_blocks):
    return jnp.einsum(
        "vsab,skcb->skvac", vectors, right_blocks, preferred_element_type=jnp.float32
    ).astype(jnp.bfloat16)


def send_layout(targets, sectors, term_count, groups):
    pair_count = sectors * term_count
    capacity = 2 * pair_count // groups
    flat_targets = targets.reshape(pair_count)
    owners = flat_targets // sectors
    onehot = (owners[:, None] == jnp.arange(groups, dtype=jnp.int32)[None, :]).astype(jnp.int32)
    before = jnp.cumsum(onehot, axis=0) - onehot
    position = jnp.sum(before * onehot, axis=1)
    slot_ids = owners * capacity + position
    term_ids = jnp.tile(jnp.arange(term_count, dtype=jnp.int32), sectors)
    labels = jnp.full((groups * capacity, 2), -1, jnp.int32)
    labels = labels.at[slot_ids].set(jnp.stack([flat_targets % sectors, term_ids], axis=1))
    return (slot_ids, labels.reshape(groups, capacity, 2), capacity)


def pack_blocks(blocks, slot_ids, groups, capacity):
    filled = (
        jnp.zeros((groups * capacity,) + blocks.shape[1:], blocks.dtype).at[slot_ids].set(blocks)
    )
    return filled.reshape((groups, capacity) + blocks.shape[1:])


def left_side(arrived, labels, left_blocks):
    sectors = left_blocks.shape[0]
    term_count = left_blocks.shape[1]
    block_width = left_blocks.shape[2]
    target_ids = labels[:, 0]
    term_ids = labels[:, 1]
    pair_ids = target_ids * term_count + term_ids
    onehot = (
        pair_ids[:, None] == jnp.arange(sectors * term_count, dtype=jnp.int32)[None, :]
    ).astype(jnp.bfloat16)
    grouped = jnp.einsum(
        "pq,pvac->qvac", onehot, arrived, preferred_element_type=jnp.float32
    ).astype(jnp.bfloat16)
    lefts = left_blocks.reshape(sectors * term_count, block_width, block_width)
    result = jnp.einsum("qab,qvbc->qvac", lefts, grouped, preferred_element_type=jnp.float32)
    result = result.reshape(sectors, term_count, arrived.shape[1], block_width, block_width)
    return jnp.transpose(jnp.sum(result, axis=1), (1, 0, 2, 3))


def per_device(wavefunction, right_blocks, left_blocks, targets):
    sectors = right_blocks.shape[0]
    term_count = right_blocks.shape[1]
    block_width = right_blocks.shape[2]
    pair_count = sectors * term_count
    groups = lax.axis_size("sector")
    slot_ids, labels, capacity = send_layout(targets, sectors, term_count, groups)
    slot_total = groups * capacity
    products_both = right_products(wavefunction, right_blocks).reshape(
        pair_count, 2, block_width, block_width
    )
    arrived, got_labels = (
        lax.all_to_all(
            pack_blocks(products_both, slot_ids, groups, capacity),
            "sector",
            split_axis=0,
            concat_axis=0,
            tiled=True,
        ),
        lax.all_to_all(labels, "sector", split_axis=0, concat_axis=0, tiled=True),
    )
    partial_value = left_side(
        arrived.reshape(slot_total, 2, block_width, block_width),
        got_labels.reshape(slot_total, 2),
        left_blocks,
    )
    return lax.psum_scatter(partial_value, "op", scatter_dimension=2, tiled=True)


def solution(mesh):
    return jax.shard_map(
        per_device,
        mesh=mesh,
        in_specs=(
            P(None, "sector", None, None),
            P("sector", "op", None, None),
            P("sector", "op", None, None),
            P("sector", "op"),
        ),
        out_specs=P(None, "sector", "op", None),
        check_vma=False,
    )
```

profile of v0, /device:TPU:1, one launch (start us, length us, event | category | flops | bytes accessed | tf_op | source)
XLA Modules:
  0.0 343.2 jit_solution(5557862807757759863)
XLA Ops:
  6.5 0.0 copy-start
  6.5 0.9 reshape.157
  7.5 0.8 reshape.156
  8.2 0.1 stack_tile.3
  8.3 0.1 fusion.6
  8.4 0.1 reduce_window_sum.11
  8.5 0.2 select_reduce_fusion
  8.7 0.1 copy.19
  8.8 0.8 scatter_custom_fusion
  9.6 0.9 copy.21
  10.5 10.5 %all-to-all-start = ((s32[32,4,2]{1,2,0:T(2,128)}), s32[32,4,2]{1,2,0:T(2,128)S(1)}, u32[]{:S(2)}, u32[]{:S(2)}) async-start(s32[32,4,2]{1,2,0:T(2,128)} %copy.21), calls=%async_computation | async-start | bytes 65536 | tf_op jit(solution)/shard_map/all_to_all | solution.py:73
  21.0 0.0 copy-done
  21.0 4.2 %convolution_convert_fusion = bf16[8,8,128,2,128]{4,2,3,1,0:T(8,128)(2,1)} fusion(bf16[8,8,128,128]{3,2,1,0:T(8,128)(2,1)S(1)} %copy-done, bf16[2,8,128,128]{3,2,1,0:T(8,128)(2,1)} %param.4), kind=kOutput, calls=%fused_computation.5 | convolution fusion | flops 538968064 | bytes 6815744 | tf_op jit(solution)/shard_map/vsab,skcb->skvac/dot_general | solution.py:8
  25.2 6.3 %copy.24 = bf16[64,2,128,128]{3,2,1,0:T(8,128)(2,1)} copy(bf16[64,2,128,128]{2,3,1,0:T(8,128)(2,1)} %bitcast.46) | data formatting | bytes 8388608 | tf_op jit(solution)/shard_map/reshape | solution.py:62
  31.6 5.3 %broadcast_in_dim.5 = bf16[128,2,128,128]{3,2,1,0:T(8,128)(2,1)} broadcast(bf16[]{:T(256)} %constant.42.clone.1), dimensions={} | broadcast | bytes 8388610 | tf_op jit(solution)/shard_map/broadcast_in_dim | solution.py:30
  36.9 12.0 %scatter_fusion = bf16[128,2,128,128]{3,2,1,0:T(8,128)(2,1)} fusion(bf16[128,2,128,128]{3,2,1,0:T(8,128)(2,1)} %broadcast_in_dim.5, s32[64]{0:T(128)S(1)} %get-tuple-element.6, bf16[64,2,128,128]{3,2,1,0:T(8,128)(2,1)} %copy.24), kind=kCustom, calls=%fused_computation.1 | custom fusion | bytes 12583168 | tf_op jit(solution)/shard_map/scatter | solution.py:30
  48.9 11.0 %copy.25 = bf16[32,4,2,128,128]{4,1,3,2,0:T(4,128)(2,1)} copy(bf16[32,4,2,128,128]{4,3,2,1,0:T(8,128)(2,1)} %bitcast.44) | data formatting | bytes 16777216 | tf_op jit(solution)/shard_map/reshape | solution.py:32
  59.9 0.0 all-to-all-done
  59.9 9.3 %all-to-all-start.1 = ((bf16[32,4,2,128,128]{4,1,3,2,0:T(4,128)(2,1)}), bf16[32,4,2,128,128]{4,1,3,2,0:T(4,128)(2,1)}, u32[]{:S(2)}, u32[]{:S(2)}) async-start(bf16[32,4,2,128,128]{4,1,3,2,0:T(4,128)(2,1)} %copy.25), calls=%async_computation.1 | async-start | bytes 16777216 | tf_op jit(solution)/shard_map/all_to_all | solution.py:66
  69.2 0.2 reduce-scatter.2.cloned.1.call-start
  69.5 0.1 reshape.159
  69.6 182.8 %all-to-all-done.1 = bf16[32,4,2,128,128]{4,1,3,2,0:T(4,128)(2,1)} async-done(((bf16[32,4,2,128,128]{4,1,3,2,0:T(4,128)(2,1)}), bf16[32,4,2,128,128]{4,1,3,2,0:T(4,128)(2,1)}, u32[]{:S(2)}, u32[]{:S(2)}) %all-to-all-start.1) | async-done | bytes 8388640 | tf_op jit(solution)/shard_map/all_to_all | solution.py:66
  252.4 6.2 %copy.26 = bf16[32,4,2,128,128]{4,1,0,3,2:T(4,128)(2,1)S(1)} copy(bf16[32,4,2,128,128]{4,1,3,2,0:T(4,128)(2,1)} %all-to-all-done.1) | data formatting | bytes 16777216 | tf_op jit(solution)/shard_map/all_to_all | solution.py:66
  258.6 0.0 copy-start.1
  258.6 1.2 convolution_convert_fusion.1
  259.9 0.3 copy-done.1
  260.2 7.1 %bitcast_reduce_fusion = f32[8,2,128,128]{2,3,1,0:T(8,128)S(1)} fusion(bf16[64,128,128,1]{2,1,3,0:T(8,128)(2,1)S(1)} %bitcast.49, bf16[64,2,128,128]{3,0,2,1:T(8,128)(2,1)S(1)} %convolution_convert_fusion.1), kind=kOutput, calls=%fused_computation.2 | convolution fusion | flops 538705920 | bytes 7340032 | tf_op jit(solution)/shard_map/qab,qvbc->qvac/dot_general | solution.py:49
  267.3 1.4 copy.28
  268.7 0.0 reduce-scatter.2.cloned.1.call-update
  268.7 66.2 %reduce-scatter.2.cloned.1.call-done = f32[2,8,8,128]{3,1,0,2:T(8,128)} async-done(((f32[2,8,128,128]{3,1,0,2:T(8,128)}), f32[2,8,8,128]{3,1,0,2:T(8,128)}) %reduce-scatter.2.cloned.1.call-update) | async-done | bytes 65552 | tf_op jit(solution)/shard_map/reduce_scatter | solution.py:80
  334.8 1.5 copy.29
  (6 shorter events, 0.0 us)
Async XLA Ops:
  6.5 14.5 %copy-start = (bf16[8,8,128,128]{3,2,1,0:T(8,128)(2,1)S(1)}, bf16[8,8,128,128]{3,2,1,0:T(8,128)(2,1)}, u32[]{:S(2)}) copy-start(bf16[8,8,128,128]{3,2,1,0:T(8,128)(2,1)} %param.5) | copy-start | bytes 6291460
  10.5 49.4 %all-to-all-start = ((s32[32,4,2]{1,2,0:T(2,128)}), s32[32,4,2]{1,2,0:T(2,128)S(1)}, u32[]{:S(2)}, u32[]{:S(2)}) async-start(s32[32,4,2]{1,2,0:T(2,128)} %copy.21), calls=%async_computation | async-start | bytes 65536 | tf_op jit(solution)/shard_map/all_to_all | solution.py:73
  59.9 192.5 %all-to-all-start.1 = ((bf16[32,4,2,128,128]{4,1,3,2,0:T(4,128)(2,1)}), bf16[32,4,2,128,128]{4,1,3,2,0:T(4,128)(2,1)}, u32[]{:S(2)}, u32[]{:S(2)}) async-start(bf16[32,4,2,128,128]{4,1,3,2,0:T(4,128)(2,1)} %copy.25), calls=%async_computation.1 | async-start | bytes 16777216 | tf_op jit(solution)/shard_map/all_to_all | solution.py:66
  69.2 265.6 %reduce-scatter.2.cloned.1.call-start = ((), (), s32[]{:S(2)}) async-start(), calls=%async_computation.3 | async-start | bytes 1114112 | tf_op jit(solution)/shard_map/reduce_scatter | solution.py:80
  258.6 1.6 copy-start.1
Sparse Core Ops, SparseCore 0:
  268.8 65.9 reduce-scatter.1
where the time goes:
time: 347 us; the launch traced here: 343 us
  waiting for transfers between devices  249 us (72%)
  local copies, waits for them, and re-layouts  47.7 us (14%)
  starting transfers between devices  20 us (6%)
  between operations  13.5 us (4%)
  matrix products  12.5 us (4%)
    all_to_all x1, waiting for transfers between devices, per_device(): lax.all_to_all(pack_blocks(products_both, slot_ids, groups, capacity), 's...  183 us
    reduce_scatter x1, waiting for transfers between devices, per_device(): lax.psum_scatter(partial_value, 'op', scatter_dimension=2, tiled=True)  66.2 us
    scatter x1, local copies, waits for them, and re-layouts, pack_blocks(): jnp.zeros((groups * capacity,) + blocks.shape[1:], blocks.dtype)  12 us
    reshape x1, local copies, waits for them, and re-layouts, pack_blocks(): return filled.reshape((groups, capacity) + blocks.shape[1:])  11 us
    all_to_all x1, starting transfers between devices, per_device(): lax.all_to_all(labels, 'sector', split_axis=0, concat_axis=0, tiled=True)  10.5 us
    all_to_all x1, starting transfers between devices, per_device(): lax.all_to_all(pack_blocks(products_both, slot_ids, groups, capacity), 's...  9.31 us
    dot_general x1, matrix products, left_side(): jnp.einsum('qab,qvbc->qvac', lefts, grouped, preferred_element_type=jnp.f...  7.06 us
  transfers between devices with their start and end apart: 3, of which 2 were waited for; matrix products, arithmetic and copies ran while one was open for 11% of the time, Pallas kernels for 0%

commit v1 on v0

v1 whole, which is shorter than its diff:
```python
import functools

import jax
import jax.numpy as jnp
from jax import lax
from jax.experimental import pallas as pl
from jax.experimental.pallas import tpu as pltpu
from jax.sharding import PartitionSpec as P

X, Y, Z, CORES = 4, 8, 8, 2
CAP = 4


def z_ring():
    return [
        (z * CORES + c, ((z + 1 - 2 * c) % Z) * CORES + c) for z in range(Z) for c in range(CORES)
    ]


def core_swap():
    return [(z * CORES + c, z * CORES + 1 - c) for z in range(Z) for c in range(CORES)]


def x_shift(distance):
    return [(x * Y + y, ((x + distance) % X) * Y + y) for x in range(X) for y in range(Y)]


def pack_kernel(targets_ref, right_ref, packed_ref, counts_ref):
    groups = counts_ref.shape[0]
    sectors, terms = targets_ref.shape

    def clear(g, carry):
        counts_ref[g] = 0
        return carry

    lax.fori_loop(0, groups, clear, 0)

    def place(s, carry):
        for k in range(terms):
            owner = targets_ref[s, k] >> 3
            position = counts_ref[owner]
            counts_ref[owner] = position + 1
            packed_ref[owner * CAP + position] = right_ref[s, k]
        return carry

    lax.fori_loop(0, sectors, place, 0)


def pack(targets, right_blocks, groups):
    _, _, rows, cols = right_blocks.shape
    return pl.pallas_call(
        pack_kernel,
        out_shape=jax.ShapeDtypeStruct((groups * CAP, rows, cols), right_blocks.dtype),
        in_specs=[
            pl.BlockSpec(memory_space=pltpu.SMEM),
            pl.BlockSpec(memory_space=pltpu.VMEM),
        ],
        out_specs=pl.BlockSpec(memory_space=pltpu.VMEM),
        scratch_shapes=[pltpu.SMEM((groups,), jnp.int32)],
        compiler_params=pltpu.CompilerParams(vmem_limit_bytes=16 * 2**20),
        cost_estimate=pl.CostEstimate(flops=0, bytes_accessed=8 * 2**20, transcendentals=0),
        name="pack_blocks",
    )(targets, right_blocks)


UNROLL = 8
GROUP_BITS, SECTOR_BITS = 8, 8


def plan_kernel(*refs):
    mark_refs = refs[:X]
    plan_ref, picked_ref, label_ref, sem = refs[X:]
    me = lax.axis_index("sector")
    my_x = me // Y
    rows, cols = Y * X * 16, 128
    marks = jnp.concatenate([r[...].reshape(Y * 16, cols) for r in mark_refs])
    marks = marks.astype(jnp.float32).astype(jnp.int32)
    s = lax.broadcasted_iota(jnp.int32, (rows, cols), 0) & 15
    k = lax.broadcasted_iota(jnp.int32, (rows, cols), 1)
    mine = ((marks >> 3) == me) & (s < 8) & (k < 8)
    ones = jnp.where(mine, 1.0, 0.0)
    flags = ones.astype(jnp.bfloat16)
    i = lax.broadcasted_iota(jnp.int32, (cols, cols), 0)
    j = lax.broadcasted_iota(jnp.int32, (cols, cols), 1)
    earlier = jnp.where(i < j, 1.0, 0.0).astype(jnp.bfloat16)
    position = jnp.dot(flags, earlier, preferred_element_type=jnp.float32)
    per_row = jnp.broadcast_to(jnp.sum(ones, axis=1, keepdims=True), (rows, cols))
    per_row = per_row.astype(jnp.bfloat16)
    above = jnp.where((i > j) & ((i >> 4) == (j >> 4)), 1.0, 0.0).astype(jnp.bfloat16)
    before = [
        jnp.dot(above, per_row[n : n + cols], preferred_element_type=jnp.float32)
        for n in range(0, rows, cols)
    ]
    position = position + jnp.concatenate(before)
    label = ((s << 6) | ((marks & 7) << 3) | k).astype(jnp.float32) + 1.0
    lane = lax.broadcasted_iota(jnp.int32, (X * Y, cols), 1)
    picked = jnp.zeros((X * Y, cols), jnp.float32)
    for n in range(CAP):
        chosen = jnp.where(mine & (position == float(n)), label, 0.0)
        chosen = jnp.sum(jnp.sum(chosen.reshape(X * Y, 16, cols), axis=1), axis=1, keepdims=True)
        picked = picked + jnp.where(lane == n, chosen, 0.0)
    picked_ref[...] = picked.astype(jnp.int32) - 1
    copy = pltpu.make_async_copy(picked_ref, label_ref, sem)
    copy.start()
    copy.wait()

    def note(device, count):
        base = (((my_x - (device >> 3)) & (X - 1)) << 5) | ((device & 7) << 2)
        for n in range(CAP):
            label = label_ref[device, n]
            sector = (device << 3) | (label >> 6)
            plan_ref[count] = (((base | n) << SECTOR_BITS | sector) << GROUP_BITS) | (label & 63)
            count = count + jnp.where(label >= 0, 1, 0)
        return count

    count = lax.fori_loop(0, X * Y, note, 0)
    for extra in range(UNROLL - 1):
        plan_ref[count + extra] = 64
    plan_ref[PLAN - 1] = (count + UNROLL - 1) // UNROLL


PLAN = X * Y * CAP + 16
PICKED = X * Y * CAP


def make_plan(marks):
    return pl.pallas_call(
        plan_kernel,
        out_shape=jax.ShapeDtypeStruct((PLAN,), jnp.int32),
        in_specs=[VMEM] * X,
        out_specs=SMEM,
        scratch_shapes=[
            pltpu.VMEM((X * Y, 128), jnp.int32),
            pltpu.SMEM((X * Y, 128), jnp.int32),
            pltpu.SemaphoreType.DMA,
        ],
        compiler_params=pltpu.CompilerParams(vmem_limit_bytes=16 * 2**20),
        name="plan_slots",
    )(*marks)


def half_products(plan_ref, arrived_hbm, left_hbm, wave_of, arrived_ref, left_ref, grouped_ref, sems, pieces_here=None):
    copies = [
        pltpu.make_async_copy(arrived_hbm, arrived_ref, sems.at[0]),
        pltpu.make_async_copy(left_hbm, left_ref, sems.at[1]),
    ]
    for copy in copies:
        copy.start()
    terms = left_ref.shape[0]
    width = arrived_ref.shape[1]

    def clear(g, carry):
        for n in range(8):
            grouped_ref[g * 8 + n] = jnp.zeros((width, width), jnp.float32)
        return carry

    lax.fori_loop(0, terms // 8, clear, 0)
    for copy in copies:
        copy.wait()
    if pieces_here is not None:
        pieces_here()

    def some(step, carry):
        waves = []
        groups = []
        for i in range(UNROLL):
            entry = plan_ref[step * UNROLL + i]
            groups.append(entry & (2**GROUP_BITS - 1))
            sector = (entry >> GROUP_BITS) & (2**SECTOR_BITS - 1)
            slot = entry >> (GROUP_BITS + SECTOR_BITS)
            wave = lax.dot_general(
                wave_of(step * UNROLL + i, sector).reshape(width, width),
                arrived_ref[slot],
                (((1,), (1,)), ((), ())),
                preferred_element_type=jnp.float32,
            )
            waves.append(wave.astype(jnp.bfloat16))
        for group, wave in zip(groups, waves):
            grouped_ref[group] = grouped_ref[group] + wave.astype(jnp.float32)
        return carry

    lax.fori_loop(0, plan_ref[PLAN - 1], some, 0)


def left_sum(left_ref, grouped_ref, t):
    lefts = jnp.concatenate([left_ref[t * 8 + k] for k in range(8)], axis=1)
    groups = jnp.concatenate(
        [grouped_ref[t * 8 + k].astype(jnp.bfloat16) for k in range(8)], axis=0
    )
    return jnp.dot(lefts, groups, preferred_element_type=jnp.float32)


def own_kernel(places, plan_ref, other_plan_ref, arrived_hbm, left_hbm, *refs):
    piece_refs = refs[: len(places)]
    sums_ref, picked_ref, wave_ref, arrived_ref, left_ref, grouped_ref, sems, piece_sems = refs[
        len(places) :
    ]
    op = lax.axis_index("op")
    sign = 1 - 2 * lax.rem(op, CORES)
    copies = []
    for i, (base, step) in enumerate(places):
        piece = lax.rem(op // CORES - step * sign + Z, Z)
        copies.append(
            pltpu.make_async_copy(
                piece_refs[i],
                wave_ref.at[pl.ds(base, piece_refs[i].shape[0]), piece],
                piece_sems.at[i],
            )
        )
    for copy in copies:
        copy.start()

    def pieces_here():
        for copy in copies:
            copy.wait()

    half_products(
        plan_ref,
        arrived_hbm,
        left_hbm,
        lambda n, sector: wave_ref[sector],
        arrived_ref,
        left_ref,
        grouped_ref,
        sems,
        pieces_here,
    )

    def pick(step, carry):
        for i in range(UNROLL):
            n = step * UNROLL + i
            picked_ref[n] = wave_ref[(other_plan_ref[n] >> GROUP_BITS) & (2**SECTOR_BITS - 1)]
        return carry

    lax.fori_loop(0, other_plan_ref[PLAN - 1], pick, 0)

    def left(pair, carry):
        for j in range(2):
            sums_ref[pair * 2 + j] = left_sum(left_ref, grouped_ref, pair * 2 + j)
        return carry

    lax.fori_loop(0, 4, left, 0)


def other_kernel(
    plan_ref,
    arrived_hbm,
    left_hbm,
    picked_hbm,
    sums_hbm,
    out_ref,
    arrived_ref,
    left_ref,
    grouped_ref,
    sems,
    picked_ref,
    sums_ref,
    more_sems,
):
    copies = [
        pltpu.make_async_copy(picked_hbm, picked_ref, more_sems.at[0]),
        pltpu.make_async_copy(sums_hbm, sums_ref, more_sems.at[1]),
    ]
    for copy in copies:
        copy.start()

    def more_here():
        for copy in copies:
            copy.wait()

    half_products(
        plan_ref,
        arrived_hbm,
        left_hbm,
        lambda n, sector: picked_ref[n],
        arrived_ref,
        left_ref,
        grouped_ref,
        sems,
        more_here,
    )
    width = sums_ref.shape[2]

    def left(pair, carry):
        both = []
        for j in range(2):
            t = pair * 2 + j
            total = sums_ref[t] + left_sum(left_ref, grouped_ref, t)
            both.append(total.reshape(16, 8, width))
        rows = jnp.stack(both, axis=1).reshape(16, 16, width)
        out_ref[:, pl.ds(pl.multiple_of(pair * 16, 16), 16), :] = rows.astype(out_ref.dtype)
        return carry

    lax.fori_loop(0, 4, left, 0)


SMEM = pl.BlockSpec(memory_space=pltpu.SMEM)
VMEM = pl.BlockSpec(memory_space=pltpu.VMEM)
HBM = pl.BlockSpec(memory_space=pl.ANY)


def work_space(arrived, left):
    slots, width, _ = arrived.shape
    terms = left.shape[0]
    return [
        pltpu.VMEM((slots, width, width), jnp.bfloat16),
        pltpu.VMEM((terms, width, width), jnp.bfloat16),
        pltpu.VMEM((terms + 1, width, width), jnp.float32),
        pltpu.SemaphoreType.DMA((2,)),
    ]


COST = pl.CostEstimate(flops=2 * 128 * 128**3, bytes_accessed=16 * 2**20, transcendentals=0)


def own_products(plan, other_plan, arrived, left, pieces):
    width = arrived.shape[1]
    count = len(pieces)
    return pl.pallas_call(
        functools.partial(own_kernel, [p[1:] for p in pieces]),
        out_shape=(
            jax.ShapeDtypeStruct((8, width, width), jnp.float32),
            jax.ShapeDtypeStruct((PICKED, Z, 16, width), jnp.bfloat16),
        ),
        in_specs=[SMEM, SMEM] + [HBM] * (2 + count),
        out_specs=(VMEM, VMEM),
        scratch_shapes=[pltpu.VMEM((X * Y * 8, Z, 16, width), jnp.bfloat16)]
        + work_space(arrived, left)
        + [pltpu.SemaphoreType.DMA((count,))],
        compiler_params=pltpu.CompilerParams(vmem_limit_bytes=60 * 2**20),
        cost_estimate=COST,
        name="own_products",
    )(plan, other_plan, arrived, left, *[p[0] for p in pieces])


def other_products(plan, arrived, left, picked, sums):
    width = arrived.shape[1]
    return pl.pallas_call(
        other_kernel,
        out_shape=jax.ShapeDtypeStruct((16, 64, width), jnp.bfloat16),
        in_specs=[SMEM, HBM, HBM, HBM, HBM],
        out_specs=VMEM,
        scratch_shapes=work_space(arrived, left)
        + [
            pltpu.VMEM(picked.shape, picked.dtype),
            pltpu.VMEM(sums.shape, sums.dtype),
            pltpu.SemaphoreType.DMA((2,)),
        ],
        compiler_params=pltpu.CompilerParams(vmem_limit_bytes=32 * 2**20),
        cost_estimate=COST,
        name="other_products",
    )(plan, arrived, left, picked, sums)


def spread_column(wavefunction, targets):
    op = lax.axis_index("op")
    _, sectors, rows, cols = wavefunction.shape
    piece = lax.dynamic_slice(
        wavefunction, (op % CORES, 0, (op // CORES) * 16, 0), (1, sectors, 16, cols)
    )
    marks = jnp.pad(targets.astype(jnp.bfloat16), ((0, 16 - sectors), (0, cols - targets.shape[1])))
    load = jnp.concatenate([piece, marks[None, None]], axis=1)
    columns = [[x * Y + y for y in range(Y)] for x in range(X)]
    return lax.all_to_all(
        jnp.broadcast_to(load, (Y,) + load.shape[1:]),
        "sector",
        split_axis=0,
        concat_axis=0,
        axis_index_groups=columns,
        tiled=True,
    )


def per_device(wavefunction, right_blocks, left_blocks, targets):
    sectors, terms, width, _ = right_blocks.shape
    pairs = sectors * terms
    groups = lax.axis_size("sector")
    swap = functools.partial(lax.ppermute, axis_name="op", perm=core_swap())
    ring = functools.partial(lax.ppermute, axis_name="op", perm=z_ring())
    tie = lax.optimization_barrier
    packed = pack(targets, right_blocks, groups)
    column = spread_column(wavefunction, targets)
    columns = [column] + [lax.ppermute(column, "sector", x_shift(d)) for d in range(1, X)]
    packed, *columns = tie((packed, *columns))
    arrived = lax.all_to_all(packed, "sector", split_axis=0, concat_axis=0, tiled=True)
    own_left = left_blocks.reshape(pairs, width, width)

    size = Y * sectors
    own_plan = make_plan([c[:, sectors] for c in columns])
    blocks = [c[:, :sectors].reshape(size, 16, width) for c in columns]
    chains = [[jnp.concatenate(blocks[:2])], [jnp.concatenate(blocks[2:])]]
    for step in range(1, Z):
        for chain in chains:
            chain.append(ring(chain[-1]))
        if step == 1:
            chains[0][1], own_plan, own_left = tie((chains[0][1], own_plan, own_left))
            other_plan = swap(own_plan)
            other_left = swap(own_left)
        if step == 4:
            chains[0][4], other_plan, other_left = tie((chains[0][4], other_plan, other_left))
    pieces = []
    for base, chain in ((0, chains[0]), (2 * size, chains[1])):
        pieces += [(block, base, step) for step, block in enumerate(chain)]

    arrived, *_ = tie((arrived, chains[0][-1], chains[1][-1]))
    other_arrived = swap(arrived)
    sums, picked = own_products(own_plan, other_plan, arrived, own_left, pieces)
    partial_value = other_products(other_plan, other_arrived, other_left, picked, sums)
    got = lax.all_to_all(partial_value, "op", split_axis=0, concat_axis=0, tiled=True)
    return jnp.sum(got.reshape(Z, CORES, 8, 8, width).astype(jnp.float32), axis=0)


def solution(mesh):
    return jax.shard_map(
        per_device,
        mesh=mesh,
        in_specs=(
            P(None, "sector", None, None),
            P("sector", "op", None, None),
            P("sector", "op", None, None),
            P("sector", "op"),
        ),
        out_specs=P(None, "sector", "op", None),
        check_vma=False,
    )
```

time: 347 us -> 198 us (0.57)
  the two profiles are of different devices: /device:TPU:1 before, /device:TPU:15 now
where the time goes in v1:
time: 198 us; the launch traced here: 197 us
  starting transfers between devices  108 us (55%)
  blocking collectives  31.7 us (16%)
  Pallas kernels  27.7 us (14%)
  waiting for transfers between devices  18.3 us (9%)
  local copies, waits for them, and re-layouts  9.57 us (5%)
    ppermute x14, starting transfers between devices, per_device(): chain.append(ring(chain[-1]))  72 us
    all_to_all x1, blocking collectives, per_device(): lax.all_to_all(partial_value, 'op', split_axis=0, concat_axis=0, tiled=True)  16.1 us
    all_to_all x1, blocking collectives, spread_column(): lax.all_to_all(jnp.broadcast_to(load, (Y,) + load.shape[1:]), 'sector', s...  15.6 us
    ppermute x14, waiting for transfers between devices, per_device(): chain.append(ring(chain[-1]))  15.3 us
    pallas_call x1, Pallas kernels, own_products(): pl.pallas_call(functools.partial(own_kernel, [p[1:] for p in pieces]), ou...  14.5 us
    all_to_all x1, starting transfers between devices, per_device(): lax.all_to_all(packed, 'sector', split_axis=0, concat_axis=0, tiled=True)  11.2 us
    pallas_call x1, Pallas kernels, other_products(): pl.pallas_call(other_kernel, out_shape=jax.ShapeDtypeStruct((16, 64, widt...  9.38 us
    unnamed x50, local copies, waits for them, and re-layouts  9.35 us
  transfers between devices with their start and end apart: 21, of which 14 were waited for; matrix products, arithmetic and copies ran while one was open for 0% of the time, Pallas kernels for 9%

profile of v1, /device:TPU:15, one launch (start us, length us, event | category | flops | bytes accessed | tf_op | source)
XLA Modules:
  0.0 197.2 jit_solution(3477969696241578119)
XLA Ops:
  1.1 15.6 %all_to_all.15 = bf16[8,9,16,128]{3,2,1,0:T(8,128)(2,1)S(1)} all-to-all(bf16[8,9,16,128]{3,2,1,0:T(8,128)(2,1)S(1)} %broadcast_in_dim.12), channel_id=1, replica_groups={{0,16,32,48,64,80,96,112},{128,144,160,176,192,208,224,240},{256,272,28..., dimensions={0} | all-to-all | bytes 589824 | tf_op jit(solution)/shard_map/all_to_all | solution.py:364
  16.8 2.5 %collective-permute-start.2 = (bf16[8,9,16,128]{3,2,0,1:T(8,128)(2,1)S(1)}, bf16[8,9,16,128]{3,2,0,1:T(8,128)(2,1)S(1)}, u32[]{:S(2)}, u32[]{:S(2)}) collective-permute-start(bf16[8,9,16,128]{3,2,0,1:T(8,128)(2,1)S(1)} %copy.9), channel_id=1, source_target_pairs={{0,384},{16,400},{32,416},{48,432},{64,448},{80,464},{96,480},{112... | collective-permute-start | bytes 884744 | tf_op jit(solution)/shard_map/ppermute | solution.py:383
  19.2 2.5 %collective-permute-start.1 = (bf16[8,9,16,128]{3,2,0,1:T(8,128)(2,1)S(1)}, bf16[8,9,16,128]{3,2,0,1:T(8,128)(2,1)S(1)}, u32[]{:S(2)}, u32[]{:S(2)}) collective-permute-start(bf16[8,9,16,128]{3,2,0,1:T(8,128)(2,1)S(1)} %copy.9), channel_id=1, source_target_pairs={{0,256},{16,272},{32,288},{48,304},{64,320},{80,336},{96,352},{112... | collective-permute-start | bytes 884744 | tf_op jit(solution)/shard_map/ppermute | solution.py:383
  21.7 4.0 %collective-permute-start = (bf16[8,9,16,128]{3,2,0,1:T(8,128)(2,1)S(1)}, bf16[8,9,16,128]{3,2,0,1:T(8,128)(2,1)S(1)}, u32[]{:S(2)}, u32[]{:S(2)}) collective-permute-start(bf16[8,9,16,128]{3,2,0,1:T(8,128)(2,1)S(1)} %copy.9), channel_id=1, source_target_pairs={{0,128},{16,144},{32,160},{48,176},{64,192},{80,208},{96,224},{112... | collective-permute-start | bytes 884744 | tf_op jit(solution)/shard_map/ppermute | solution.py:383
  29.1 2.0 %copy-done.1 = bf16[128,128,128]{2,1,0:T(8,128)(2,1)} copy-done((bf16[128,128,128]{2,1,0:T(8,128)(2,1)}, bf16[128,128,128]{2,1,0:T(8,128)(2,1)S(1)}, u32[]{:S(2)}) %copy-start.1) | copy-done | bytes 4194328
  31.7 2.5 %collective-permute-done = bf16[8,9,16,128]{3,2,0,1:T(8,128)(2,1)S(1)} collective-permute-done((bf16[8,9,16,128]{3,2,0,1:T(8,128)(2,1)S(1)}, bf16[8,9,16,128]{3,2,0,1:T(8,128)(2,1)S(1)}, u32[]{:S(2)}, u32[]{:S(2)}) %collective-permute-start) | collective-permute-done | bytes 294944 | tf_op jit(solution)/shard_map/ppermute | solution.py:383
  34.2 11.2 %all-to-all-start.1 = ((bf16[128,128,128]{2,1,0:T(8,128)(2,1)}), bf16[128,128,128]{2,1,0:T(8,128)(2,1)}, u32[]{:S(2)}, u32[]{:S(2)}) async-start(bf16[128,128,128]{2,1,0:T(8,128)(2,1)} %copy-done.1), calls=%async_computation.1 | async-start | bytes 8388608 | tf_op jit(solution)/shard_map/all_to_all | solution.py:385
  45.6 10.8 %collective-permute-start.3 = (bf16[128,16,128]{2,1,0:T(8,128)(2,1)S(1)}, bf16[128,16,128]{2,1,0:T(8,128)(2,1)S(1)}, u32[]{:S(2)}, u32[]{:S(2)}) collective-permute-start(bf16[128,16,128]{2,1,0:T(8,128)(2,1)S(1)} %pad_maximum_fusion.refs_0_), channel_id=1, source_target_pairs={{0,2},{1,15},{2,4},{3,1},{4,6},{5,3},{6,8},{7,5},{8,10},{9,7},{10,... | collective-permute-start | bytes 1572872 | tf_op jit(solution)/shard_map/ppermute | solution.py:394
  56.5 2.2 %collective-permute-start.12 = (bf16[128,16,128]{2,1,0:T(8,128)(2,1)S(1)}, bf16[128,16,128]{2,1,0:T(8,128)(2,1)S(1)}, u32[]{:S(2)}, u32[]{:S(2)}) collective-permute-start(bf16[128,16,128]{2,1,0:T(8,128)(2,1)S(1)} %pad_maximum_fusion.1.refs_8_), channel_id=1, source_target_pairs={{0,2},{1,15},{2,4},{3,1},{4,6},{5,3},{6,8},{7,5},{8,10},{9,7},{10,... | collective-permute-start | bytes 1572872 | tf_op jit(solution)/shard_map/ppermute | solution.py:394
  58.7 2.7 %plan_slots.1.plan_ref = s32[144]{0:T(256)S(1)} custom-call(bf16[8,16,128]{2,1,0:T(8,128)(2,1)S(1)} %slice_bitcast_fusion.refs_0_, bf16[8,16,128]{2,1,0:T(8,128)(2,1)S(1)} %slice_bitcast_fusion.3.refs_1_, bf16[8,16,128]{2,1,0:T(8,128)(2,1)S(1)} %get-tuple-element.34.refs_2_, bf16[8,16,128]{2,1,0:T(8,128)(2,1)S(1)} %get-tuple-element.33.refs_3_), custom_call_target="tpu_custom_call" | custom-call | tf_op jit(solution)/shard_map/plan_slots/pallas_call | solution.py:127
  62.5 5.0 %collective-permute-start.8 = (bf16[64,128,128]{2,1,0:T(8,128)(2,1)S(1)}, bf16[64,128,128]{2,1,0:T(8,128)(2,1)S(1)}, u32[]{:S(2)}, u32[]{:S(2)}) collective-permute-start(bf16[64,128,128]{2,1,0:T(8,128)(2,1)S(1)} %bitcast.20), channel_id=1, source_target_pairs={{0,1},{1,0},{2,3},{3,2},{4,5},{5,4},{6,7},{7,6},{8,9},{9,8},{10,11... | collective-permute-start | bytes 6291464 | tf_op jit(solution)/shard_map/ppermute | solution.py:398
  68.1 5.4 %collective-permute-start.13 = (bf16[128,16,128]{2,1,0:T(8,128)(2,1)S(1)}, bf16[128,16,128]{2,1,0:T(8,128)(2,1)S(1)}, u32[]{:S(2)}, u32[]{:S(2)}) collective-permute-start(bf16[128,16,128]{2,1,0:T(8,128)(2,1)S(1)} %collective-permute-done.12.refs_9_), channel_id=1, source_target_pairs={{0,2},{1,15},{2,4},{3,1},{4,6},{5,3},{6,8},{7,5},{8,10},{9,7},{10,... | collective-permute-start | bytes 1572872 | tf_op jit(solution)/shard_map/ppermute | solution.py:394
  73.5 1.9 collective-permute-start.4
  75.5 4.2 %collective-permute-done.13.refs_10_ = bf16[128,16,128]{2,1,0:T(8,128)(2,1)S(1)} collective-permute-done((bf16[128,16,128]{2,1,0:T(8,128)(2,1)S(1)}, bf16[128,16,128]{2,1,0:T(8,128)(2,1)S(1)}, u32[]{:S(2)}, u32[]{:S(2)}) %collective-permute-start.13) | collective-permute-done | bytes 524320 | tf_op jit(solution)/shard_map/ppermute | solution.py:394
  79.7 5.4 %collective-permute-start.14 = (bf16[128,16,128]{2,1,0:T(8,128)(2,1)S(1)}, bf16[128,16,128]{2,1,0:T(8,128)(2,1)S(1)}, u32[]{:S(2)}, u32[]{:S(2)}) collective-permute-start(bf16[128,16,128]{2,1,0:T(8,128)(2,1)S(1)} %collective-permute-done.13.refs_10_), channel_id=1, source_target_pairs={{0,2},{1,15},{2,4},{3,1},{4,6},{5,3},{6,8},{7,5},{8,10},{9,7},{10,... | collective-permute-start | bytes 1572872 | tf_op jit(solution)/shard_map/ppermute | solution.py:394
  85.3 5.4 %collective-permute-start.5 = (bf16[128,16,128]{2,1,0:T(8,128)(2,1)S(1)}, bf16[128,16,128]{2,1,0:T(8,128)(2,1)S(1)}, u32[]{:S(2)}, u32[]{:S(2)}) collective-permute-start(bf16[128,16,128]{2,1,0:T(8,128)(2,1)S(1)} %collective-permute-done.4.refs_2_), channel_id=1, source_target_pairs={{0,2},{1,15},{2,4},{3,1},{4,6},{5,3},{6,8},{7,5},{8,10},{9,7},{10,... | collective-permute-start | bytes 1572872 | tf_op jit(solution)/shard_map/ppermute | solution.py:394
  91.2 5.4 %collective-permute-start.15 = (bf16[128,16,128]{2,1,0:T(8,128)(2,1)S(1)}, bf16[128,16,128]{2,1,0:T(8,128)(2,1)S(1)}, u32[]{:S(2)}, u32[]{:S(2)}) collective-permute-start(bf16[128,16,128]{2,1,0:T(8,128)(2,1)S(1)} %collective-permute-done.14.refs_11_), channel_id=1, source_target_pairs={{0,2},{1,15},{2,4},{3,1},{4,6},{5,3},{6,8},{7,5},{8,10},{9,7},{10,... | collective-permute-start | bytes 1572872 | tf_op jit(solution)/shard_map/ppermute | solution.py:394
  96.8 5.4 %collective-permute-start.6 = (bf16[128,16,128]{2,1,0:T(8,128)(2,1)S(1)}, bf16[128,16,128]{2,1,0:T(8,128)(2,1)S(1)}, u32[]{:S(2)}, u32[]{:S(2)}) collective-permute-start(bf16[128,16,128]{2,1,0:T(8,128)(2,1)S(1)} %collective-permute-done.5.refs_3_), channel_id=1, source_target_pairs={{0,2},{1,15},{2,4},{3,1},{4,6},{5,3},{6,8},{7,5},{8,10},{9,7},{10,... | collective-permute-start | bytes 1572872 | tf_op jit(solution)/shard_map/ppermute | solution.py:394
  102.2 3.0 %collective-permute-start.7 = (s32[144]{0:T(256)S(1)}, s32[144]{0:T(256)S(1)}, u32[]{:S(2)}, u32[]{:S(2)}) collective-permute-start(s32[144]{0:T(256)S(1)} %plan_slots.1.plan_ref), channel_id=1, source_target_pairs={{0,1},{1,0},{2,3},{3,2},{4,5},{5,4},{6,7},{7,6},{8,9},{9,8},{10,11... | collective-permute-start | bytes 1736 | tf_op jit(solution)/shard_map/ppermute | solution.py:397
  105.3 4.9 %collective-permute-start.16 = (bf16[128,16,128]{2,1,0:T(8,128)(2,1)S(1)}, bf16[128,16,128]{2,1,0:T(8,128)(2,1)S(1)}, u32[]{:S(2)}, u32[]{:S(2)}) collective-permute-start(bf16[128,16,128]{2,1,0:T(8,128)(2,1)S(1)} %collective-permute-done.15.refs_12_), channel_id=1, source_target_pairs={{0,2},{1,15},{2,4},{3,1},{4,6},{5,3},{6,8},{7,5},{8,10},{9,7},{10,... | collective-permute-start | bytes 1572872 | tf_op jit(solution)/shard_map/ppermute | solution.py:394
  110.2 3.6 %collective-permute-start.9 = (bf16[128,16,128]{2,1,0:T(8,128)(2,1)S(1)}, bf16[128,16,128]{2,1,0:T(8,128)(2,1)S(1)}, u32[]{:S(2)}, u32[]{:S(2)}) collective-permute-start(bf16[128,16,128]{2,1,0:T(8,128)(2,1)S(1)} %collective-permute-done.6.refs_4_), channel_id=1, source_target_pairs={{0,2},{1,15},{2,4},{3,1},{4,6},{5,3},{6,8},{7,5},{8,10},{9,7},{10,... | collective-permute-start | bytes 1572872 | tf_op jit(solution)/shard_map/ppermute | solution.py:394
  113.8 2.5 %collective-permute-done.16.refs_13_ = bf16[128,16,128]{2,1,0:T(8,128)(2,1)S(1)} collective-permute-done((bf16[128,16,128]{2,1,0:T(8,128)(2,1)S(1)}, bf16[128,16,128]{2,1,0:T(8,128)(2,1)S(1)}, u32[]{:S(2)}, u32[]{:S(2)}) %collective-permute-start.16) | collective-permute-done | bytes 524320 | tf_op jit(solution)/shard_map/ppermute | solution.py:394
  116.2 5.4 %collective-permute-start.17 = (bf16[128,16,128]{2,1,0:T(8,128)(2,1)S(1)}, bf16[128,16,128]{2,1,0:T(8,128)(2,1)S(1)}, u32[]{:S(2)}, u32[]{:S(2)}) collective-permute-start(bf16[128,16,128]{2,1,0:T(8,128)(2,1)S(1)} %collective-permute-done.16.refs_13_), channel_id=1, source_target_pairs={{0,2},{1,15},{2,4},{3,1},{4,6},{5,3},{6,8},{7,5},{8,10},{9,7},{10,... | collective-permute-start | bytes 1572872 | tf_op jit(solution)/shard_map/ppermute | solution.py:394
  121.9 5.4 %collective-permute-start.10 = (bf16[128,16,128]{2,1,0:T(8,128)(2,1)S(1)}, bf16[128,16,128]{2,1,0:T(8,128)(2,1)S(1)}, u32[]{:S(2)}, u32[]{:S(2)}) collective-permute-start(bf16[128,16,128]{2,1,0:T(8,128)(2,1)S(1)} %collective-permute-done.9.refs_5_), channel_id=1, source_target_pairs={{0,2},{1,15},{2,4},{3,1},{4,6},{5,3},{6,8},{7,5},{8,10},{9,7},{10,... | collective-permute-start | bytes 1572872 | tf_op jit(solution)/shard_map/ppermute | solution.py:394
  127.8 5.4 %collective-permute-start.18 = (bf16[128,16,128]{2,1,0:T(8,128)(2,1)S(1)}, bf16[128,16,128]{2,1,0:T(8,128)(2,1)S(1)}, u32[]{:S(2)}, u32[]{:S(2)}) collective-permute-start(bf16[128,16,128]{2,1,0:T(8,128)(2,1)S(1)} %collective-permute-done.17.refs_14_), channel_id=1, source_target_pairs={{0,2},{1,15},{2,4},{3,1},{4,6},{5,3},{6,8},{7,5},{8,10},{9,7},{10,... | collective-permute-start | bytes 1572872 | tf_op jit(solution)/shard_map/ppermute | solution.py:394
  133.4 5.4 %collective-permute-start.11 = (bf16[128,16,128]{2,1,0:T(8,128)(2,1)S(1)}, bf16[128,16,128]{2,1,0:T(8,128)(2,1)}, u32[]{:S(2)}, u32[]{:S(2)}) collective-permute-start(bf16[128,16,128]{2,1,0:T(8,128)(2,1)S(1)} %collective-permute-done.10.refs_6_), channel_id=1, source_target_pairs={{0,2},{1,15},{2,4},{3,1},{4,6},{5,3},{6,8},{7,5},{8,10},{9,7},{10,... | collective-permute-start | bytes 1572872 | tf_op jit(solution)/shard_map/ppermute | solution.py:394
  140.1 4.8 %collective-permute-done.11.refs_7_ = bf16[128,16,128]{2,1,0:T(8,128)(2,1)} collective-permute-done((bf16[128,16,128]{2,1,0:T(8,128)(2,1)S(1)}, bf16[128,16,128]{2,1,0:T(8,128)(2,1)}, u32[]{:S(2)}, u32[]{:S(2)}) %collective-permute-start.11) | collective-permute-done | bytes 524320 | tf_op jit(solution)/shard_map/ppermute | solution.py:394
  144.9 7.6 %collective-permute-start.19 = (bf16[128,128,128]{2,1,0:T(8,128)(2,1)}, bf16[128,128,128]{2,1,0:T(8,128)(2,1)}, u32[]{:S(2)}, u32[]{:S(2)}) collective-permute-start(bf16[128,128,128]{2,1,0:T(8,128)(2,1)} %all-to-all-done.1.arrived_hbm), channel_id=1, source_target_pairs={{0,1},{1,0},{2,3},{3,2},{4,5},{5,4},{6,7},{7,6},{8,9},{9,8},{10,11... | collective-permute-start | bytes 12582920 | tf_op jit(solution)/shard_map/ppermute | solution.py:406
  152.6 14.5 %own_products.1 = (f32[8,128,128]{2,1,0:T(8,128)}, bf16[128,8,16,128]{3,2,1,0:T(8,128)(2,1)}) custom-call(s32[144]{0:T(256)} %copy-done.6, s32[144]{0:T(256)} %copy-done.7, bf16[128,128,128]{2,1,0:T(8,128)(2,1)} %all-to-all-done.1.arrived_hbm, bf16[64,128,128]{2,1,0:T(8,128)(2,1)} %bitcast.19, bf16[128,16,128]{2,1,0:T(8,128)(2,1)} %copy-done.9, ...), custom_call_target="tpu_custom_call" | custom-call | flops 536870912 | bytes 16777216 | tf_op jit(solution)/shard_map/own_products/pallas_call | solution.py:319
  167.1 2.2 %copy-done.2 = bf16[128,8,16,128]{3,2,1,0:T(8,128)(2,1)S(1)} copy-done((bf16[128,8,16,128]{3,2,1,0:T(8,128)(2,1)S(1)}, bf16[128,8,16,128]{3,2,1,0:T(8,128)(2,1)}, u32[]{:S(2)}) %copy-start.2) | copy-done | bytes 4194328
  171.0 9.4 %other_products.1 = bf16[16,64,128]{2,1,0:T(8,128)(2,1)S(1)} custom-call(s32[144]{0:T(256)S(1)} %copy-done.8, bf16[128,128,128]{2,1,0:T(8,128)(2,1)} %collective-permute-done.19.arrived_hbm, bf16[64,128,128]{2,1,0:T(8,128)(2,1)S(1)} %collective-permute-done.8.left_hbm, bf16[128,8,16,128]{3,2,1,0:T(8,128)(2,1)S(1)} %copy-done.2, f32[8,128,128]{2,1,0:T(8,128)S(1)} %copy-done.4), custom_call_target="tpu_custom_call" | custom-call | flops 536870912 | bytes 16777216 | tf_op jit(solution)/shard_map/other_products/pallas_call | solution.py:338
  180.4 16.1 %all_to_all.16 = bf16[16,64,128]{2,1,0:T(8,128)(2,1)S(1)} all-to-all(bf16[16,64,128]{2,1,0:T(8,128)(2,1)S(1)} %other_products.1), channel_id=1, replica_groups=mesh['sector'=32,'op'=16] {'op'}, dimensions={0} | all-to-all | bytes 524288 | tf_op jit(solution)/shard_map/all_to_all | solution.py:409
  (85 shorter events, 12.4 us)
Async XLA Ops:
  16.8 14.4 %collective-permute-start.2 = (bf16[8,9,16,128]{3,2,0,1:T(8,128)(2,1)S(1)}, bf16[8,9,16,128]{3,2,0,1:T(8,128)(2,1)S(1)}, u32[]{:S(2)}, u32[]{:S(2)}) collective-permute-start(bf16[8,9,16,128]{3,2,0,1:T(8,128)(2,1)S(1)} %copy.9), channel_id=1, source_target_pairs={{0,384},{16,400},{32,416},{48,432},{64,448},{80,464},{96,480},{112... | collective-permute-start | bytes 884744 | tf_op jit(solution)/shard_map/ppermute | solution.py:383
  19.2 12.4 %collective-permute-start.1 = (bf16[8,9,16,128]{3,2,0,1:T(8,128)(2,1)S(1)}, bf16[8,9,16,128]{3,2,0,1:T(8,128)(2,1)S(1)}, u32[]{:S(2)}, u32[]{:S(2)}) collective-permute-start(bf16[8,9,16,128]{3,2,0,1:T(8,128)(2,1)S(1)} %copy.9), channel_id=1, source_target_pairs={{0,256},{16,272},{32,288},{48,304},{64,320},{80,336},{96,352},{112... | collective-permute-start | bytes 884744 | tf_op jit(solution)/shard_map/ppermute | solution.py:383
  21.7 12.4 %collective-permute-start = (bf16[8,9,16,128]{3,2,0,1:T(8,128)(2,1)S(1)}, bf16[8,9,16,128]{3,2,0,1:T(8,128)(2,1)S(1)}, u32[]{:S(2)}, u32[]{:S(2)}) collective-permute-start(bf16[8,9,16,128]{3,2,0,1:T(8,128)(2,1)S(1)} %copy.9), channel_id=1, source_target_pairs={{0,128},{16,144},{32,160},{48,176},{64,192},{80,208},{96,224},{112... | collective-permute-start | bytes 884744 | tf_op jit(solution)/shard_map/ppermute | solution.py:383
  34.2 110.8 %all-to-all-start.1 = ((bf16[128,128,128]{2,1,0:T(8,128)(2,1)}), bf16[128,128,128]{2,1,0:T(8,128)(2,1)}, u32[]{:S(2)}, u32[]{:S(2)}) async-start(bf16[128,128,128]{2,1,0:T(8,128)(2,1)} %copy-done.1), calls=%async_computation.1 | async-start | bytes 8388608 | tf_op jit(solution)/shard_map/all_to_all | solution.py:385
  45.6 107.0 %copy-start.9 = (bf16[128,16,128]{2,1,0:T(8,128)(2,1)}, bf16[128,16,128]{2,1,0:T(8,128)(2,1)S(1)}, u32[]{:S(2)}) copy-start(bf16[128,16,128]{2,1,0:T(8,128)(2,1)S(1)} %pad_maximum_fusion.refs_0_) | copy-start | bytes 1572868
  45.6 16.9 %collective-permute-start.3 = (bf16[128,16,128]{2,1,0:T(8,128)(2,1)S(1)}, bf16[128,16,128]{2,1,0:T(8,128)(2,1)S(1)}, u32[]{:S(2)}, u32[]{:S(2)}) collective-permute-start(bf16[128,16,128]{2,1,0:T(8,128)(2,1)S(1)} %pad_maximum_fusion.refs_0_), channel_id=1, source_target_pairs={{0,2},{1,15},{2,4},{3,1},{4,6},{5,3},{6,8},{7,5},{8,10},{9,7},{10,... | collective-permute-start | bytes 1572872 | tf_op jit(solution)/shard_map/ppermute | solution.py:394
  56.5 53.7 %copy-start.10 = (bf16[128,16,128]{2,1,0:T(8,128)(2,1)}, bf16[128,16,128]{2,1,0:T(8,128)(2,1)S(1)}, u32[]{:S(2)}) copy-start(bf16[128,16,128]{2,1,0:T(8,128)(2,1)S(1)} %pad_maximum_fusion.1.refs_8_) | copy-start | bytes 1572868
  56.5 11.6 %collective-permute-start.12 = (bf16[128,16,128]{2,1,0:T(8,128)(2,1)S(1)}, bf16[128,16,128]{2,1,0:T(8,128)(2,1)S(1)}, u32[]{:S(2)}, u32[]{:S(2)}) collective-permute-start(bf16[128,16,128]{2,1,0:T(8,128)(2,1)S(1)} %pad_maximum_fusion.1.refs_8_), channel_id=1, source_target_pairs={{0,2},{1,15},{2,4},{3,1},{4,6},{5,3},{6,8},{7,5},{8,10},{9,7},{10,... | collective-permute-start | bytes 1572872 | tf_op jit(solution)/shard_map/ppermute | solution.py:394
  61.4 91.1 %copy-start.6 = (s32[144]{0:T(256)}, s32[144]{0:T(256)S(1)}, u32[]{:S(2)}) copy-start(s32[144]{0:T(256)S(1)} %plan_slots.1.plan_ref) | copy-start | bytes 1732
  62.5 51.3 %copy-start.12 = (bf16[128,16,128]{2,1,0:T(8,128)(2,1)}, bf16[128,16,128]{2,1,0:T(8,128)(2,1)S(1)}, u32[]{:S(2)}) copy-start(bf16[128,16,128]{2,1,0:T(8,128)(2,1)S(1)} %collective-permute-done.3.refs_1_) | copy-start | bytes 1572868
  62.5 47.7 %collective-permute-start.8 = (bf16[64,128,128]{2,1,0:T(8,128)(2,1)S(1)}, bf16[64,128,128]{2,1,0:T(8,128)(2,1)S(1)}, u32[]{:S(2)}, u32[]{:S(2)}) collective-permute-start(bf16[64,128,128]{2,1,0:T(8,128)(2,1)S(1)} %bitcast.20), channel_id=1, source_target_pairs={{0,1},{1,0},{2,3},{3,2},{4,5},{5,4},{6,7},{7,6},{8,9},{9,8},{10,11... | collective-permute-start | bytes 6291464 | tf_op jit(solution)/shard_map/ppermute | solution.py:398
  68.1 48.1 %copy-start.13 = (bf16[128,16,128]{2,1,0:T(8,128)(2,1)}, bf16[128,16,128]{2,1,0:T(8,128)(2,1)S(1)}, u32[]{:S(2)}) copy-start(bf16[128,16,128]{2,1,0:T(8,128)(2,1)S(1)} %collective-permute-done.12.refs_9_) | copy-start | bytes 1572868
  68.1 11.5 %collective-permute-start.13 = (bf16[128,16,128]{2,1,0:T(8,128)(2,1)S(1)}, bf16[128,16,128]{2,1,0:T(8,128)(2,1)S(1)}, u32[]{:S(2)}, u32[]{:S(2)}) collective-permute-start(bf16[128,16,128]{2,1,0:T(8,128)(2,1)S(1)} %collective-permute-done.12.refs_9_), channel_id=1, source_target_pairs={{0,2},{1,15},{2,4},{3,1},{4,6},{5,3},{6,8},{7,5},{8,10},{9,7},{10,... | collective-permute-start | bytes 1572872 | tf_op jit(solution)/shard_map/ppermute | solution.py:394
  73.5 11.7 %collective-permute-start.4 = (bf16[128,16,128]{2,1,0:T(8,128)(2,1)S(1)}, bf16[128,16,128]{2,1,0:T(8,128)(2,1)S(1)}, u32[]{:S(2)}, u32[]{:S(2)}) collective-permute-start(bf16[128,16,128]{2,1,0:T(8,128)(2,1)S(1)} %collective-permute-done.3.refs_1_), channel_id=1, source_target_pairs={{0,2},{1,15},{2,4},{3,1},{4,6},{5,3},{6,8},{7,5},{8,10},{9,7},{10,... | collective-permute-start | bytes 1572872 | tf_op jit(solution)/shard_map/ppermute | solution.py:394
  79.6 42.0 %copy-start.14 = (bf16[128,16,128]{2,1,0:T(8,128)(2,1)}, bf16[128,16,128]{2,1,0:T(8,128)(2,1)S(1)}, u32[]{:S(2)}) copy-start(bf16[128,16,128]{2,1,0:T(8,128)(2,1)S(1)} %collective-permute-done.13.refs_10_) | copy-start | bytes 1572868
  79.7 11.5 %collective-permute-start.14 = (bf16[128,16,128]{2,1,0:T(8,128)(2,1)S(1)}, bf16[128,16,128]{2,1,0:T(8,128)(2,1)S(1)}, u32[]{:S(2)}, u32[]{:S(2)}) collective-permute-start(bf16[128,16,128]{2,1,0:T(8,128)(2,1)S(1)} %collective-permute-done.13.refs_10_), channel_id=1, source_target_pairs={{0,2},{1,15},{2,4},{3,1},{4,6},{5,3},{6,8},{7,5},{8,10},{9,7},{10,... | collective-permute-start | bytes 1572872 | tf_op jit(solution)/shard_map/ppermute | solution.py:394
  85.3 36.6 %copy-start.15 = (bf16[128,16,128]{2,1,0:T(8,128)(2,1)}, bf16[128,16,128]{2,1,0:T(8,128)(2,1)S(1)}, u32[]{:S(2)}) copy-start(bf16[128,16,128]{2,1,0:T(8,128)(2,1)S(1)} %collective-permute-done.4.refs_2_) | copy-start | bytes 1572868
  85.3 11.5 %collective-permute-start.5 = (bf16[128,16,128]{2,1,0:T(8,128)(2,1)S(1)}, bf16[128,16,128]{2,1,0:T(8,128)(2,1)S(1)}, u32[]{:S(2)}, u32[]{:S(2)}) collective-permute-start(bf16[128,16,128]{2,1,0:T(8,128)(2,1)S(1)} %collective-permute-done.4.refs_2_), channel_id=1, source_target_pairs={{0,2},{1,15},{2,4},{3,1},{4,6},{5,3},{6,8},{7,5},{8,10},{9,7},{10,... | collective-permute-start | bytes 1572872 | tf_op jit(solution)/shard_map/ppermute | solution.py:394
  91.2 36.1 %copy-start.16 = (bf16[128,16,128]{2,1,0:T(8,128)(2,1)}, bf16[128,16,128]{2,1,0:T(8,128)(2,1)S(1)}, u32[]{:S(2)}) copy-start(bf16[128,16,128]{2,1,0:T(8,128)(2,1)S(1)} %collective-permute-done.14.refs_11_) | copy-start | bytes 1572868
  91.2 14.1 %collective-permute-start.15 = (bf16[128,16,128]{2,1,0:T(8,128)(2,1)S(1)}, bf16[128,16,128]{2,1,0:T(8,128)(2,1)S(1)}, u32[]{:S(2)}, u32[]{:S(2)}) collective-permute-start(bf16[128,16,128]{2,1,0:T(8,128)(2,1)S(1)} %collective-permute-done.14.refs_11_), channel_id=1, source_target_pairs={{0,2},{1,15},{2,4},{3,1},{4,6},{5,3},{6,8},{7,5},{8,10},{9,7},{10,... | collective-permute-start | bytes 1572872 | tf_op jit(solution)/shard_map/ppermute | solution.py:394
  96.8 31.0 %copy-start.17 = (bf16[128,16,128]{2,1,0:T(8,128)(2,1)}, bf16[128,16,128]{2,1,0:T(8,128)(2,1)S(1)}, u32[]{:S(2)}) copy-start(bf16[128,16,128]{2,1,0:T(8,128)(2,1)S(1)} %collective-permute-done.5.refs_3_) | copy-start | bytes 1572868
  96.8 13.4 %collective-permute-start.6 = (bf16[128,16,128]{2,1,0:T(8,128)(2,1)S(1)}, bf16[128,16,128]{2,1,0:T(8,128)(2,1)S(1)}, u32[]{:S(2)}, u32[]{:S(2)}) collective-permute-start(bf16[128,16,128]{2,1,0:T(8,128)(2,1)S(1)} %collective-permute-done.5.refs_3_), channel_id=1, source_target_pairs={{0,2},{1,15},{2,4},{3,1},{4,6},{5,3},{6,8},{7,5},{8,10},{9,7},{10,... | collective-permute-start | bytes 1572872 | tf_op jit(solution)/shard_map/ppermute | solution.py:394
  102.2 7.9 %collective-permute-start.7 = (s32[144]{0:T(256)S(1)}, s32[144]{0:T(256)S(1)}, u32[]{:S(2)}, u32[]{:S(2)}) collective-permute-start(s32[144]{0:T(256)S(1)} %plan_slots.1.plan_ref), channel_id=1, source_target_pairs={{0,1},{1,0},{2,3},{3,2},{4,5},{5,4},{6,7},{7,6},{8,9},{9,8},{10,11... | collective-permute-start | bytes 1736 | tf_op jit(solution)/shard_map/ppermute | solution.py:397
  105.3 27.9 %copy-start.18 = (bf16[128,16,128]{2,1,0:T(8,128)(2,1)}, bf16[128,16,128]{2,1,0:T(8,128)(2,1)S(1)}, u32[]{:S(2)}) copy-start(bf16[128,16,128]{2,1,0:T(8,128)(2,1)S(1)} %collective-permute-done.15.refs_12_) | copy-start | bytes 1572868
  105.3 11.0 %collective-permute-start.16 = (bf16[128,16,128]{2,1,0:T(8,128)(2,1)S(1)}, bf16[128,16,128]{2,1,0:T(8,128)(2,1)S(1)}, u32[]{:S(2)}, u32[]{:S(2)}) collective-permute-start(bf16[128,16,128]{2,1,0:T(8,128)(2,1)S(1)} %collective-permute-done.15.refs_12_), channel_id=1, source_target_pairs={{0,2},{1,15},{2,4},{3,1},{4,6},{5,3},{6,8},{7,5},{8,10},{9,7},{10,... | collective-permute-start | bytes 1572872 | tf_op jit(solution)/shard_map/ppermute | solution.py:394
  110.1 42.4 %copy-start.7 = (s32[144]{0:T(256)}, s32[144]{0:T(256)S(1)}, u32[]{:S(2)}) copy-start(s32[144]{0:T(256)S(1)} %collective-permute-done.7.other_plan_ref.plan_ref) | copy-start | bytes 1732
  110.2 11.7 %collective-permute-start.9 = (bf16[128,16,128]{2,1,0:T(8,128)(2,1)S(1)}, bf16[128,16,128]{2,1,0:T(8,128)(2,1)S(1)}, u32[]{:S(2)}, u32[]{:S(2)}) collective-permute-start(bf16[128,16,128]{2,1,0:T(8,128)(2,1)S(1)} %collective-permute-done.6.refs_4_), channel_id=1, source_target_pairs={{0,2},{1,15},{2,4},{3,1},{4,6},{5,3},{6,8},{7,5},{8,10},{9,7},{10,... | collective-permute-start | bytes 1572872 | tf_op jit(solution)/shard_map/ppermute | solution.py:394
  116.2 11.5 %collective-permute-start.17 = (bf16[128,16,128]{2,1,0:T(8,128)(2,1)S(1)}, bf16[128,16,128]{2,1,0:T(8,128)(2,1)S(1)}, u32[]{:S(2)}, u32[]{:S(2)}) collective-permute-start(bf16[128,16,128]{2,1,0:T(8,128)(2,1)S(1)} %collective-permute-done.16.refs_13_), channel_id=1, source_target_pairs={{0,2},{1,15},{2,4},{3,1},{4,6},{5,3},{6,8},{7,5},{8,10},{9,7},{10,... | collective-permute-start | bytes 1572872 | tf_op jit(solution)/shard_map/ppermute | solution.py:394
  121.9 11.5 %collective-permute-start.10 = (bf16[128,16,128]{2,1,0:T(8,128)(2,1)S(1)}, bf16[128,16,128]{2,1,0:T(8,128)(2,1)S(1)}, u32[]{:S(2)}, u32[]{:S(2)}) collective-permute-start(bf16[128,16,128]{2,1,0:T(8,128)(2,1)S(1)} %collective-permute-done.9.refs_5_), channel_id=1, source_target_pairs={{0,2},{1,15},{2,4},{3,1},{4,6},{5,3},{6,8},{7,5},{8,10},{9,7},{10,... | collective-permute-start | bytes 1572872 | tf_op jit(solution)/shard_map/ppermute | solution.py:394
  127.8 11.5 %collective-permute-start.18 = (bf16[128,16,128]{2,1,0:T(8,128)(2,1)S(1)}, bf16[128,16,128]{2,1,0:T(8,128)(2,1)S(1)}, u32[]{:S(2)}, u32[]{:S(2)}) collective-permute-start(bf16[128,16,128]{2,1,0:T(8,128)(2,1)S(1)} %collective-permute-done.17.refs_14_), channel_id=1, source_target_pairs={{0,2},{1,15},{2,4},{3,1},{4,6},{5,3},{6,8},{7,5},{8,10},{9,7},{10,... | collective-permute-start | bytes 1572872 | tf_op jit(solution)/shard_map/ppermute | solution.py:394
  133.4 11.5 %collective-permute-start.11 = (bf16[128,16,128]{2,1,0:T(8,128)(2,1)S(1)}, bf16[128,16,128]{2,1,0:T(8,128)(2,1)}, u32[]{:S(2)}, u32[]{:S(2)}) collective-permute-start(bf16[128,16,128]{2,1,0:T(8,128)(2,1)S(1)} %collective-permute-done.10.refs_6_), channel_id=1, source_target_pairs={{0,2},{1,15},{2,4},{3,1},{4,6},{5,3},{6,8},{7,5},{8,10},{9,7},{10,... | collective-permute-start | bytes 1572872 | tf_op jit(solution)/shard_map/ppermute | solution.py:394
  144.9 22.2 %collective-permute-start.19 = (bf16[128,128,128]{2,1,0:T(8,128)(2,1)}, bf16[128,128,128]{2,1,0:T(8,128)(2,1)}, u32[]{:S(2)}, u32[]{:S(2)}) collective-permute-start(bf16[128,128,128]{2,1,0:T(8,128)(2,1)} %all-to-all-done.1.arrived_hbm), channel_id=1, source_target_pairs={{0,1},{1,0},{2,3},{3,2},{4,5},{5,4},{6,7},{7,6},{8,9},{9,8},{10,11... | collective-permute-start | bytes 12582920 | tf_op jit(solution)/shard_map/ppermute | solution.py:406
  (14 other events, 107.9 us)

commit v2 on v1

--- a/solution.py
+++ b/solution.py
@@ -11,9 +11,9 @@
 CAP = 4
 
 
-def z_ring():
+def z_shift(distance):
     return [
-        (z * CORES + c, ((z + 1 - 2 * c) % Z) * CORES + c) for z in range(Z) for c in range(CORES)
+        (z * CORES + c, ((z + distance) % Z) * CORES + c) for z in range(Z) for c in range(CORES)
     ]
 
 
@@ -63,7 +63,7 @@
     )(targets, right_blocks)
 
 
-UNROLL = 8
+UNROLL = 16
 GROUP_BITS, SECTOR_BITS = 8, 8
 
 
@@ -139,13 +139,15 @@
     )(*marks)
 
 
-def half_products(plan_ref, arrived_hbm, left_hbm, wave_of, arrived_ref, left_ref, grouped_ref, sems, pieces_here=None):
-    copies = [
-        pltpu.make_async_copy(arrived_hbm, arrived_ref, sems.at[0]),
-        pltpu.make_async_copy(left_hbm, left_ref, sems.at[1]),
-    ]
-    for copy in copies:
-        copy.start()
+def half_products(
+    plan_ref, arrived_hbm, left_hbm, wave_of, arrived_ref, left_ref, grouped_ref, sems, wait_first, wait_step, start_more=None
+):
+    arrived = pltpu.make_async_copy(arrived_hbm, arrived_ref, sems.at[0])
+    left = pltpu.make_async_copy(left_hbm, left_ref, sems.at[1])
+    arrived.start()
+    if start_more is not None:
+        start_more()
+    left.start()
     terms = left_ref.shape[0]
     width = arrived_ref.shape[1]
 
@@ -155,12 +157,11 @@
         return carry
 
     lax.fori_loop(0, terms // 8, clear, 0)
-    for copy in copies:
-        copy.wait()
-    if pieces_here is not None:
-        pieces_here()
+    wait_first()
+    arrived.wait()
 
     def some(step, carry):
+        wait_step(step)
         waves = []
         groups = []
         for i in range(UNROLL):
@@ -180,6 +181,7 @@
         return carry
 
     lax.fori_loop(0, plan_ref[PLAN - 1], some, 0)
+    left.wait()
 
 
 def left_sum(left_ref, grouped_ref, t):
@@ -192,14 +194,22 @@
 
 def own_kernel(places, plan_ref, other_plan_ref, arrived_hbm, left_hbm, *refs):
     piece_refs = refs[: len(places)]
-    sums_ref, picked_ref, wave_ref, arrived_ref, left_ref, grouped_ref, sems, piece_sems = refs[
-        len(places) :
-    ]
+    (
+        sums_ref,
+        picked_hbm,
+        picked_ref,
+        wave_ref,
+        arrived_ref,
+        left_ref,
+        grouped_ref,
+        sems,
+        piece_sems,
+        picked_sems,
+    ) = refs[len(places) :]
     op = lax.axis_index("op")
-    sign = 1 - 2 * lax.rem(op, CORES)
     copies = []
     for i, (base, step) in enumerate(places):
-        piece = lax.rem(op // CORES - step * sign + Z, Z)
+        piece = lax.rem(op // CORES - step + Z, Z)
         copies.append(
             pltpu.make_async_copy(
                 piece_refs[i],
@@ -210,9 +220,27 @@
     for copy in copies:
         copy.start()
 
+    def picked_copy(step):
+        rows = pl.ds(step * UNROLL, UNROLL)
+        return pltpu.make_async_copy(picked_ref.at[rows], picked_hbm.at[rows], picked_sems.at[step])
+
+    def pick(step, carry):
+        for i in range(UNROLL):
+            n = step * UNROLL + i
+            picked_ref[n] = wave_ref[(other_plan_ref[n] >> GROUP_BITS) & (2**SECTOR_BITS - 1)]
+        picked_copy(step).start()
+        return carry
+
+    def finish_pick(step, carry):
+        picked_copy(step).wait()
+        return carry
+
+    other_steps = other_plan_ref[PLAN - 1]
+
     def pieces_here():
         for copy in copies:
             copy.wait()
+        lax.fori_loop(0, other_steps, pick, 0)
 
     half_products(
         plan_ref,
@@ -224,15 +252,8 @@
         grouped_ref,
         sems,
         pieces_here,
-    )
-
-    def pick(step, carry):
-        for i in range(UNROLL):
-            n = step * UNROLL + i
-            picked_ref[n] = wave_ref[(other_plan_ref[n] >> GROUP_BITS) & (2**SECTOR_BITS - 1)]
-        return carry
-
-    lax.fori_loop(0, other_plan_ref[PLAN - 1], pick, 0)
+        lambda step: None,
+    )
 
     def left(pair, carry):
         for j in range(2):
@@ -240,6 +261,7 @@
         return carry
 
     lax.fori_loop(0, 4, left, 0)
+    lax.fori_loop(0, other_steps, finish_pick, 0)
 
 
 def other_kernel(
@@ -257,16 +279,23 @@
     sums_ref,
     more_sems,
 ):
-    copies = [
-        pltpu.make_async_copy(picked_hbm, picked_ref, more_sems.at[0]),
-        pltpu.make_async_copy(sums_hbm, sums_ref, more_sems.at[1]),
-    ]
-    for copy in copies:
-        copy.start()
-
-    def more_here():
-        for copy in copies:
-            copy.wait()
+    sums_copy = pltpu.make_async_copy(sums_hbm, sums_ref, more_sems.at[PICKED // UNROLL])
+    steps = plan_ref[PLAN - 1]
+
+    def picked_copy(step):
+        rows = pl.ds(step * UNROLL, UNROLL)
+        return pltpu.make_async_copy(picked_hbm.at[rows], picked_ref.at[rows], more_sems.at[step])
+
+    def start_step(step, carry):
+        picked_copy(step).start()
+        return carry
+
+    def start_more():
+        lax.fori_loop(0, steps, start_step, 0)
+        sums_copy.start()
+
+    def wait_step(step):
+        picked_copy(step).wait()
 
     half_products(
         plan_ref,
@@ -277,8 +306,11 @@
         left_ref,
         grouped_ref,
         sems,
-        more_here,
-    )
+        lambda: None,
+        wait_step,
+        start_more,
+    )
+    sums_copy.wait()
     width = sums_ref.shape[2]
 
     def left(pair, carry):
@@ -323,10 +355,16 @@
             jax.ShapeDtypeStruct((PICKED, Z, 16, width), jnp.bfloat16),
         ),
         in_specs=[SMEM, SMEM] + [HBM] * (2 + count),
-        out_specs=(VMEM, VMEM),
-        scratch_shapes=[pltpu.VMEM((X * Y * 8, Z, 16, width), jnp.bfloat16)]
+        out_specs=(VMEM, HBM),
+        scratch_shapes=[
+            pltpu.VMEM((PICKED, Z, 16, width), jnp.bfloat16),
+            pltpu.VMEM((X * Y * 8, Z, 16, width), jnp.bfloat16),
+        ]
         + work_space(arrived, left)
-        + [pltpu.SemaphoreType.DMA((count,))],
+        + [
+            pltpu.SemaphoreType.DMA((count,)),
+            pltpu.SemaphoreType.DMA((PICKED // UNROLL,)),
+        ],
         compiler_params=pltpu.CompilerParams(vmem_limit_bytes=60 * 2**20),
         cost_estimate=COST,
         name="own_products",
@@ -344,9 +382,9 @@
         + [
             pltpu.VMEM(picked.shape, picked.dtype),
             pltpu.VMEM(sums.shape, sums.dtype),
-            pltpu.SemaphoreType.DMA((2,)),
+            pltpu.SemaphoreType.DMA((PICKED // UNROLL + 1,)),
         ],
-        compiler_params=pltpu.CompilerParams(vmem_limit_bytes=32 * 2**20),
+        compiler_params=pltpu.CompilerParams(vmem_limit_bytes=60 * 2**20),
         cost_estimate=COST,
         name="other_products",
     )(plan, arrived, left, picked, sums)
@@ -376,33 +414,45 @@
     pairs = sectors * terms
     groups = lax.axis_size("sector")
     swap = functools.partial(lax.ppermute, axis_name="op", perm=core_swap())
-    ring = functools.partial(lax.ppermute, axis_name="op", perm=z_ring())
+    ring_up = functools.partial(lax.ppermute, axis_name="op", perm=z_shift(1))
+    ring_down = functools.partial(lax.ppermute, axis_name="op", perm=z_shift(-1))
     tie = lax.optimization_barrier
     packed = pack(targets, right_blocks, groups)
     column = spread_column(wavefunction, targets)
     columns = [column] + [lax.ppermute(column, "sector", x_shift(d)) for d in range(1, X)]
-    packed, *columns = tie((packed, *columns))
+    packed, *_ = tie((packed, *columns))
     arrived = lax.all_to_all(packed, "sector", split_axis=0, concat_axis=0, tiled=True)
     own_left = left_blocks.reshape(pairs, width, width)
 
     size = Y * sectors
     own_plan = make_plan([c[:, sectors] for c in columns])
     blocks = [c[:, :sectors].reshape(size, 16, width) for c in columns]
-    chains = [[jnp.concatenate(blocks[:2])], [jnp.concatenate(blocks[2:])]]
-    for step in range(1, Z):
-        for chain in chains:
-            chain.append(ring(chain[-1]))
-        if step == 1:
-            chains[0][1], own_plan, own_left = tie((chains[0][1], own_plan, own_left))
-            other_plan = swap(own_plan)
+    starts = [jnp.concatenate(blocks[:2]), jnp.concatenate(blocks[2:])]
+    ups = [[s] for s in starts]
+    downs = [[s] for s in starts]
+    for step in range(1, Z // 2):
+        for chain in ups:
+            chain.append(ring_up(chain[-1]))
+        for chain in downs:
+            chain.append(ring_down(chain[-1]))
+        if step == 2:
+            ups[1][2], own_left = tie((ups[1][2], own_left))
             other_left = swap(own_left)
-        if step == 4:
-            chains[0][4], other_plan, other_left = tie((chains[0][4], other_plan, other_left))
+        if step == 3:
+            ups[0][3], other_plan = tie((ups[0][3], swap(own_plan)))
     pieces = []
-    for base, chain in ((0, chains[0]), (2 * size, chains[1])):
-        pieces += [(block, base, step) for step, block in enumerate(chain)]
-
-    arrived, *_ = tie((arrived, chains[0][-1], chains[1][-1]))
+    last = []
+    for n, start in enumerate(starts):
+        base = 2 * size * n
+        pieces.append((start, base, 0))
+        for step in range(1, Z // 2):
+            pieces.append((ups[n][step], base, step))
+            pieces.append((downs[n][step], base, -step))
+        last.append((ring_up(ups[n][-1][:size]), base, Z // 2))
+        last.append((ring_down(downs[n][-1][size:]), base + size, Z // 2))
+    pieces += last
+
+    arrived, *_ = tie((arrived, *[p[0] for p in last]))
     other_arrived = swap(arrived)
     sums, picked = own_products(own_plan, other_plan, arrived, own_left, pieces)
     partial_value = other_products(other_plan, other_arrived, other_left, picked, sums)

time: 198 us -> 190 us (0.960)
  the two profiles are of different devices: /device:TPU:15 before, /device:TPU:1 now
where the time goes in v2:
time: 190 us; the launch traced here: 189 us
  starting transfers between devices  92.5 us (49%)
  blocking collectives  40.2 us (21%)
  waiting for transfers between devices  24.2 us (13%)
  Pallas kernels  21.6 us (11%)
  local copies, waits for them, and re-layouts  7.96 us (4%)
    ppermute x6, starting transfers between devices, per_device(): chain.append(ring_down(chain[-1]))  31.5 us
    all_to_all x1, blocking collectives, per_device(): lax.all_to_all(partial_value, 'op', split_axis=0, concat_axis=0, tiled=True)  22.6 us
    all_to_all x1, blocking collectives, spread_column(): lax.all_to_all(jnp.broadcast_to(load, (Y,) + load.shape[1:]), 'sector', s...  17.6 us
    ppermute x6, waiting for transfers between devices, per_device(): chain.append(ring_up(chain[-1]))  16.4 us
    ppermute x6, starting transfers between devices, per_device(): chain.append(ring_up(chain[-1]))  13.6 us
    ppermute x3, starting transfers between devices, per_device(): lax.ppermute(column, 'sector', x_shift(d))  11.2 us
    pallas_call x1, Pallas kernels, own_products(): pl.pallas_call(functools.partial(own_kernel, [p[1:] for p in pieces]), ou...  10.7 us
    ppermute x2, starting transfers between devices, per_device(): last.append((ring_down(downs[n][-1][size:]), base + size, Z // 2))  9.15 us
  transfers between devices with their start and end apart: 23, of which 8 were waited for; matrix products, arithmetic and copies ran while one was open for 1% of the time, Pallas kernels for 8%

profile of v2, /device:TPU:1, one launch (start us, length us, event | category | flops | bytes accessed | tf_op | source)
XLA Modules:
  0.0 188.7 jit_solution(211071351547032268)
XLA Ops:
  1.1 17.6 %all_to_all.15 = bf16[8,9,16,128]{3,2,1,0:T(8,128)(2,1)S(1)} all-to-all(bf16[8,9,16,128]{3,2,1,0:T(8,128)(2,1)S(1)} %broadcast_in_dim.12), channel_id=1, replica_groups={{0,16,32,48,64,80,96,112},{128,144,160,176,192,208,224,240},{256,272,28..., dimensions={0} | all-to-all | bytes 589824 | tf_op jit(solution)/shard_map/all_to_all | solution.py:402
  18.8 3.8 %collective-permute-start = (bf16[8,9,16,128]{3,2,0,1:T(8,128)(2,1)S(1)}, bf16[8,9,16,128]{3,2,0,1:T(8,128)(2,1)S(1)}, u32[]{:S(2)}, u32[]{:S(2)}) collective-permute-start(bf16[8,9,16,128]{3,2,0,1:T(8,128)(2,1)S(1)} %copy.9), channel_id=1, source_target_pairs={{0,128},{16,144},{32,160},{48,176},{64,192},{80,208},{96,224},{112... | collective-permute-start | bytes 884744 | tf_op jit(solution)/shard_map/ppermute | solution.py:422
  22.6 4.4 %collective-permute-start.4 = (bf16[8,9,16,128]{3,2,0,1:T(8,128)(2,1)S(1)}, bf16[8,9,16,128]{3,2,0,1:T(8,128)(2,1)S(1)}, u32[]{:S(2)}, u32[]{:S(2)}) collective-permute-start(bf16[8,9,16,128]{3,2,0,1:T(8,128)(2,1)S(1)} %copy.9), channel_id=1, source_target_pairs={{0,256},{16,272},{32,288},{48,304},{64,320},{80,336},{96,352},{112... | collective-permute-start | bytes 884744 | tf_op jit(solution)/shard_map/ppermute | solution.py:422
  26.9 3.1 %collective-permute-start.5 = (bf16[8,9,16,128]{3,2,0,1:T(8,128)(2,1)S(1)}, bf16[8,9,16,128]{3,2,0,1:T(8,128)(2,1)S(1)}, u32[]{:S(2)}, u32[]{:S(2)}) collective-permute-start(bf16[8,9,16,128]{3,2,0,1:T(8,128)(2,1)S(1)} %copy.9), channel_id=1, source_target_pairs={{0,384},{16,400},{32,416},{48,432},{64,448},{80,464},{96,480},{112... | collective-permute-start | bytes 884744 | tf_op jit(solution)/shard_map/ppermute | solution.py:422
  33.4 2.0 %copy-done.1 = bf16[128,128,128]{2,1,0:T(8,128)(2,1)} copy-done((bf16[128,128,128]{2,1,0:T(8,128)(2,1)}, bf16[128,128,128]{2,1,0:T(8,128)(2,1)S(1)}, u32[]{:S(2)}) %copy-start.1) | copy-done | bytes 4194328
  35.4 2.3 %collective-permute-done.5 = bf16[8,9,16,128]{3,2,0,1:T(8,128)(2,1)S(1)} collective-permute-done((bf16[8,9,16,128]{3,2,0,1:T(8,128)(2,1)S(1)}, bf16[8,9,16,128]{3,2,0,1:T(8,128)(2,1)S(1)}, u32[]{:S(2)}, u32[]{:S(2)}) %collective-permute-start.5) | collective-permute-done | bytes 294944 | tf_op jit(solution)/shard_map/ppermute | solution.py:422
  37.8 8.1 %all-to-all-start.1 = ((bf16[128,128,128]{2,1,0:T(8,128)(2,1)}), bf16[128,128,128]{2,1,0:T(8,128)(2,1)}, u32[]{:S(2)}, u32[]{:S(2)}) async-start(bf16[128,128,128]{2,1,0:T(8,128)(2,1)} %copy-done.1), calls=%async_computation.1 | async-start | bytes 8388608 | tf_op jit(solution)/shard_map/all_to_all | solution.py:424
  46.1 4.0 %collective-permute-start.12 = (bf16[128,16,128]{2,1,0:T(8,128)(2,1)S(1)}, bf16[128,16,128]{2,1,0:T(8,128)(2,1)S(1)}, u32[]{:S(2)}, u32[]{:S(2)}) collective-permute-start(bf16[128,16,128]{2,1,0:T(8,128)(2,1)S(1)} %pad_maximum_fusion.1.refs_7_), channel_id=1, source_target_pairs={{0,2},{1,3},{2,4},{3,5},{4,6},{5,7},{6,8},{7,9},{8,10},{9,11},{10,... | collective-permute-start | bytes 1572872 | tf_op jit(solution)/shard_map/ppermute | solution.py:435
  50.1 8.6 %collective-permute-start.16 = (bf16[128,16,128]{2,1,0:T(8,128)(2,1)S(1)}, bf16[128,16,128]{2,1,0:T(8,128)(2,1)S(1)}, u32[]{:S(2)}, u32[]{:S(2)}) collective-permute-start(bf16[128,16,128]{2,1,0:T(8,128)(2,1)S(1)} %pad_maximum_fusion.1.refs_7_), channel_id=1, source_target_pairs={{0,14},{1,15},{2,0},{3,1},{4,2},{5,3},{6,4},{7,5},{8,6},{9,7},{10,... | collective-permute-start | bytes 1572872 | tf_op jit(solution)/shard_map/ppermute | solution.py:437
  58.8 1.9 %collective-permute-start.1 = (bf16[128,16,128]{2,1,0:T(8,128)(2,1)S(1)}, bf16[128,16,128]{2,1,0:T(8,128)(2,1)S(1)}, u32[]{:S(2)}, u32[]{:S(2)}) collective-permute-start(bf16[128,16,128]{2,1,0:T(8,128)(2,1)S(1)} %pad_maximum_fusion.refs_0_), channel_id=1, source_target_pairs={{0,2},{1,3},{2,4},{3,5},{4,6},{5,7},{6,8},{7,9},{8,10},{9,11},{10,... | collective-permute-start | bytes 1572872 | tf_op jit(solution)/shard_map/ppermute | solution.py:435
  60.7 4.6 %collective-permute-start.8 = (bf16[128,16,128]{2,1,0:T(8,128)(2,1)S(1)}, bf16[128,16,128]{2,1,0:T(8,128)(2,1)S(1)}, u32[]{:S(2)}, u32[]{:S(2)}) collective-permute-start(bf16[128,16,128]{2,1,0:T(8,128)(2,1)S(1)} %pad_maximum_fusion.refs_0_), channel_id=1, source_target_pairs={{0,14},{1,15},{2,0},{3,1},{4,2},{5,3},{6,4},{7,5},{8,6},{9,7},{10,... | collective-permute-start | bytes 1572872 | tf_op jit(solution)/shard_map/ppermute | solution.py:437
  65.3 2.3 %collective-permute-done.12.refs_8_ = bf16[128,16,128]{2,1,0:T(8,128)(2,1)S(1)} collective-permute-done((bf16[128,16,128]{2,1,0:T(8,128)(2,1)S(1)}, bf16[128,16,128]{2,1,0:T(8,128)(2,1)S(1)}, u32[]{:S(2)}, u32[]{:S(2)}) %collective-permute-start.12) | collective-permute-done | bytes 524320 | tf_op jit(solution)/shard_map/ppermute | solution.py:435
  69.6 4.6 %collective-permute-start.17 = (bf16[128,16,128]{2,1,0:T(8,128)(2,1)S(1)}, bf16[128,16,128]{2,1,0:T(8,128)(2,1)S(1)}, u32[]{:S(2)}, u32[]{:S(2)}) collective-permute-start(bf16[128,16,128]{2,1,0:T(8,128)(2,1)S(1)} %collective-permute-done.16.refs_9_), channel_id=1, source_target_pairs={{0,14},{1,15},{2,0},{3,1},{4,2},{5,3},{6,4},{7,5},{8,6},{9,7},{10,... | collective-permute-start | bytes 1572872 | tf_op jit(solution)/shard_map/ppermute | solution.py:437
  74.2 4.7 %collective-permute-done.1.refs_1_ = bf16[128,16,128]{2,1,0:T(8,128)(2,1)S(1)} collective-permute-done((bf16[128,16,128]{2,1,0:T(8,128)(2,1)S(1)}, bf16[128,16,128]{2,1,0:T(8,128)(2,1)S(1)}, u32[]{:S(2)}, u32[]{:S(2)}) %collective-permute-start.1) | collective-permute-done | bytes 524320 | tf_op jit(solution)/shard_map/ppermute | solution.py:435
  80.8 4.6 %collective-permute-start.9 = (bf16[128,16,128]{2,1,0:T(8,128)(2,1)S(1)}, bf16[128,16,128]{2,1,0:T(8,128)(2,1)S(1)}, u32[]{:S(2)}, u32[]{:S(2)}) collective-permute-start(bf16[128,16,128]{2,1,0:T(8,128)(2,1)S(1)} %collective-permute-done.8.refs_2_), channel_id=1, source_target_pairs={{0,14},{1,15},{2,0},{3,1},{4,2},{5,3},{6,4},{7,5},{8,6},{9,7},{10,... | collective-permute-start | bytes 1572872 | tf_op jit(solution)/shard_map/ppermute | solution.py:437
  85.4 4.7 %collective-permute-done.13.refs_10_ = bf16[128,16,128]{2,1,0:T(8,128)(2,1)S(1)} collective-permute-done((bf16[128,16,128]{2,1,0:T(8,128)(2,1)S(1)}, bf16[128,16,128]{2,1,0:T(8,128)(2,1)S(1)}, u32[]{:S(2)}, u32[]{:S(2)}) %collective-permute-start.13) | collective-permute-done | bytes 524320 | tf_op jit(solution)/shard_map/ppermute | solution.py:435
  92.1 4.6 %collective-permute-start.18 = (bf16[128,16,128]{2,1,0:T(8,128)(2,1)S(1)}, bf16[128,16,128]{2,1,0:T(8,128)(2,1)S(1)}, u32[]{:S(2)}, u32[]{:S(2)}) collective-permute-start(bf16[128,16,128]{2,1,0:T(8,128)(2,1)S(1)} %collective-permute-done.17.refs_11_), channel_id=1, source_target_pairs={{0,14},{1,15},{2,0},{3,1},{4,2},{5,3},{6,4},{7,5},{8,6},{9,7},{10,... | collective-permute-start | bytes 1572872 | tf_op jit(solution)/shard_map/ppermute | solution.py:437
  96.6 4.6 %collective-permute-done.2.refs_3_ = bf16[128,16,128]{2,1,0:T(8,128)(2,1)S(1)} collective-permute-done((bf16[128,16,128]{2,1,0:T(8,128)(2,1)S(1)}, bf16[128,16,128]{2,1,0:T(8,128)(2,1)S(1)}, u32[]{:S(2)}, u32[]{:S(2)}) %collective-permute-start.2) | collective-permute-done | bytes 524320 | tf_op jit(solution)/shard_map/ppermute | solution.py:435
  103.2 4.6 %collective-permute-start.10 = (bf16[128,16,128]{2,1,0:T(8,128)(2,1)S(1)}, bf16[128,16,128]{2,1,0:T(8,128)(2,1)S(1)}, u32[]{:S(2)}, u32[]{:S(2)}) collective-permute-start(bf16[128,16,128]{2,1,0:T(8,128)(2,1)S(1)} %collective-permute-done.9.refs_4_), channel_id=1, source_target_pairs={{0,14},{1,15},{2,0},{3,1},{4,2},{5,3},{6,4},{7,5},{8,6},{9,7},{10,... | collective-permute-start | bytes 1572872 | tf_op jit(solution)/shard_map/ppermute | solution.py:437
  109.3 2.8 %plan_slots.1.plan_ref = s32[144]{0:T(256)S(1)} custom-call(bf16[8,16,128]{2,1,0:T(8,128)(2,1)S(1)} %slice_bitcast_fusion.3.refs_0_, bf16[8,16,128]{2,1,0:T(8,128)(2,1)S(1)} %slice_bitcast_fusion.2.refs_1_, bf16[8,16,128]{2,1,0:T(8,128)(2,1)S(1)} %slice_bitcast_fusion.1.refs_2_, bf16[8,16,128]{2,1,0:T(8,128)(2,1)S(1)} %slice_bitcast_fusion.refs_3_), custom_call_target="tpu_custom_call" | custom-call | tf_op jit(solution)/shard_map/plan_slots/pallas_call | solution.py:127
  112.1 6.2 %collective-permute-start.6 = (s32[144]{0:T(256)S(1)}, s32[144]{0:T(256)S(1)}, u32[]{:S(2)}, u32[]{:S(2)}) collective-permute-start(s32[144]{0:T(256)S(1)} %plan_slots.1.plan_ref), channel_id=1, source_target_pairs={{0,1},{1,0},{2,3},{3,2},{4,5},{5,4},{6,7},{7,6},{8,9},{9,8},{10,11... | collective-permute-start | bytes 1736 | tf_op jit(solution)/shard_map/ppermute | solution.py:442
  118.3 1.9 %collective-permute-start.15 = (bf16[64,16,128]{2,1,0:T(8,128)(2,1)S(1)}, bf16[64,16,128]{2,1,0:T(8,128)(2,1)S(1)}, u32[]{:S(2)}, u32[]{:S(2)}) collective-permute-start(bf16[64,16,128]{2,1,0:T(8,128)(2,1)S(1)} %slice.57), channel_id=1, source_target_pairs={{0,2},{1,3},{2,4},{3,5},{4,6},{5,7},{6,8},{7,9},{8,10},{9,11},{10,... | collective-permute-start | bytes 786440 | tf_op jit(solution)/shard_map/ppermute | solution.py:451
  120.3 4.6 %collective-permute-start.19 = (bf16[64,16,128]{2,1,0:T(8,128)(2,1)S(1)}, bf16[64,16,128]{2,1,0:T(8,128)(2,1)S(1)}, u32[]{:S(2)}, u32[]{:S(2)}) collective-permute-start(bf16[64,16,128]{2,1,0:T(8,128)(2,1)S(1)} %slice.58), channel_id=1, source_target_pairs={{0,14},{1,15},{2,0},{3,1},{4,2},{5,3},{6,4},{7,5},{8,6},{9,7},{10,... | collective-permute-start | bytes 786440 | tf_op jit(solution)/shard_map/ppermute | solution.py:452
  125.0 1.9 %collective-permute-start.7 = (bf16[64,16,128]{2,1,0:T(8,128)(2,1)S(1)}, bf16[64,16,128]{2,1,0:T(8,128)(2,1)S(1)}, u32[]{:S(2)}, u32[]{:S(2)}) collective-permute-start(bf16[64,16,128]{2,1,0:T(8,128)(2,1)S(1)} %slice.42), channel_id=1, source_target_pairs={{0,2},{1,3},{2,4},{3,5},{4,6},{5,7},{6,8},{7,9},{8,10},{9,11},{10,... | collective-permute-start | bytes 786440 | tf_op jit(solution)/shard_map/ppermute | solution.py:451
  127.7 4.6 %collective-permute-start.11 = (bf16[64,16,128]{2,1,0:T(8,128)(2,1)S(1)}, bf16[64,16,128]{2,1,0:T(8,128)(2,1)}, u32[]{:S(2)}, u32[]{:S(2)}) collective-permute-start(bf16[64,16,128]{2,1,0:T(8,128)(2,1)S(1)} %slice.54), channel_id=1, source_target_pairs={{0,14},{1,15},{2,0},{3,1},{4,2},{5,3},{6,4},{7,5},{8,6},{9,7},{10,... | collective-permute-start | bytes 786440 | tf_op jit(solution)/shard_map/ppermute | solution.py:452
  132.4 2.0 %collective-permute-done.7.refs_14_ = bf16[64,16,128]{2,1,0:T(8,128)(2,1)S(1)} collective-permute-done((bf16[64,16,128]{2,1,0:T(8,128)(2,1)S(1)}, bf16[64,16,128]{2,1,0:T(8,128)(2,1)S(1)}, u32[]{:S(2)}, u32[]{:S(2)}) %collective-permute-start.7) | collective-permute-done | bytes 262176 | tf_op jit(solution)/shard_map/ppermute | solution.py:451
  135.6 3.0 %all-to-all-done.1.arrived_hbm = bf16[128,128,128]{2,1,0:T(8,128)(2,1)} async-done(((bf16[128,128,128]{2,1,0:T(8,128)(2,1)}), bf16[128,128,128]{2,1,0:T(8,128)(2,1)}, u32[]{:S(2)}, u32[]{:S(2)}) %all-to-all-start.1) | async-done | bytes 4194336 | tf_op jit(solution)/shard_map/all_to_all | solution.py:424
  138.6 7.2 %collective-permute-start.20 = (bf16[128,128,128]{2,1,0:T(8,128)(2,1)}, bf16[128,128,128]{2,1,0:T(8,128)(2,1)}, u32[]{:S(2)}, u32[]{:S(2)}) collective-permute-start(bf16[128,128,128]{2,1,0:T(8,128)(2,1)} %all-to-all-done.1.arrived_hbm), channel_id=1, source_target_pairs={{0,1},{1,0},{2,3},{3,2},{4,5},{5,4},{6,7},{7,6},{8,9},{9,8},{10,11... | collective-permute-start | bytes 12582920 | tf_op jit(solution)/shard_map/ppermute | solution.py:456
  145.7 1.9 %collective-permute-start.21 = (bf16[64,128,128]{2,1,0:T(8,128)(2,1)}, bf16[64,128,128]{2,1,0:T(8,128)(2,1)}, u32[]{:S(2)}, u32[]{:S(2)}) collective-permute-start(bf16[64,128,128]{2,1,0:T(8,128)(2,1)} %bitcast.20), channel_id=1, source_target_pairs={{0,1},{1,0},{2,3},{3,2},{4,5},{5,4},{6,7},{7,6},{8,9},{9,8},{10,11... | collective-permute-start | bytes 6291464 | tf_op jit(solution)/shard_map/ppermute | solution.py:440
  147.8 10.7 %own_products.1 = (f32[8,128,128]{2,1,0:T(8,128)}, bf16[128,8,16,128]{3,2,1,0:T(8,128)(2,1)}) custom-call(s32[144]{0:T(256)} %copy-done.4, s32[144]{0:T(256)} %copy-done.26, bf16[128,128,128]{2,1,0:T(8,128)(2,1)} %all-to-all-done.1.arrived_hbm, bf16[64,128,128]{2,1,0:T(8,128)(2,1)} %bitcast.21, bf16[128,16,128]{2,1,0:T(8,128)(2,1)} %copy-done.8, ...), custom_call_target="tpu_custom_call" | custom-call | flops 536870912 | bytes 16777216 | tf_op jit(solution)/shard_map/own_products/pallas_call | solution.py:351
  158.5 6.9 %other_products.1 = bf16[16,64,128]{2,1,0:T(8,128)(2,1)} custom-call(s32[144]{0:T(256)} %copy-done.26, bf16[128,128,128]{2,1,0:T(8,128)(2,1)} %collective-permute-done.20.arrived_hbm, bf16[64,128,128]{2,1,0:T(8,128)(2,1)} %collective-permute-done.21.left_hbm, bf16[128,8,16,128]{3,2,1,0:T(8,128)(2,1)} %get-tuple-element.19.picked_hbm, ...), custom_call_target="tpu_custom_call" | custom-call | flops 536870912 | bytes 16777216 | tf_op jit(solution)/shard_map/other_products/pallas_call | solution.py:376
  165.5 22.6 %all_to_all.16 = bf16[16,64,128]{2,1,0:T(8,128)(2,1)S(1)} all-to-all(bf16[16,64,128]{2,1,0:T(8,128)(2,1)} %other_products.1), channel_id=1, replica_groups=mesh['sector'=32,'op'=16] {'op'}, dimensions={0} | all-to-all | bytes 524288 | tf_op jit(solution)/shard_map/all_to_all | solution.py:459
  (99 shorter events, 16.8 us)
Async XLA Ops:
  18.8 16.7 %collective-permute-start = (bf16[8,9,16,128]{3,2,0,1:T(8,128)(2,1)S(1)}, bf16[8,9,16,128]{3,2,0,1:T(8,128)(2,1)S(1)}, u32[]{:S(2)}, u32[]{:S(2)}) collective-permute-start(bf16[8,9,16,128]{3,2,0,1:T(8,128)(2,1)S(1)} %copy.9), channel_id=1, source_target_pairs={{0,128},{16,144},{32,160},{48,176},{64,192},{80,208},{96,224},{112... | collective-permute-start | bytes 884744 | tf_op jit(solution)/shard_map/ppermute | solution.py:422
  22.6 12.9 %collective-permute-start.4 = (bf16[8,9,16,128]{3,2,0,1:T(8,128)(2,1)S(1)}, bf16[8,9,16,128]{3,2,0,1:T(8,128)(2,1)S(1)}, u32[]{:S(2)}, u32[]{:S(2)}) collective-permute-start(bf16[8,9,16,128]{3,2,0,1:T(8,128)(2,1)S(1)} %copy.9), channel_id=1, source_target_pairs={{0,256},{16,272},{32,288},{48,304},{64,320},{80,336},{96,352},{112... | collective-permute-start | bytes 884744 | tf_op jit(solution)/shard_map/ppermute | solution.py:422
  26.9 10.8 %collective-permute-start.5 = (bf16[8,9,16,128]{3,2,0,1:T(8,128)(2,1)S(1)}, bf16[8,9,16,128]{3,2,0,1:T(8,128)(2,1)S(1)}, u32[]{:S(2)}, u32[]{:S(2)}) collective-permute-start(bf16[8,9,16,128]{3,2,0,1:T(8,128)(2,1)S(1)} %copy.9), channel_id=1, source_target_pairs={{0,384},{16,400},{32,416},{48,432},{64,448},{80,464},{96,480},{112... | collective-permute-start | bytes 884744 | tf_op jit(solution)/shard_map/ppermute | solution.py:422
  37.8 100.8 %all-to-all-start.1 = ((bf16[128,128,128]{2,1,0:T(8,128)(2,1)}), bf16[128,128,128]{2,1,0:T(8,128)(2,1)}, u32[]{:S(2)}, u32[]{:S(2)}) async-start(bf16[128,128,128]{2,1,0:T(8,128)(2,1)} %copy-done.1), calls=%async_computation.1 | async-start | bytes 8388608 | tf_op jit(solution)/shard_map/all_to_all | solution.py:424
  45.9 39.5 %copy-start.6 = (bf16[8,9,16,128]{3,2,1,0:T(8,128)(2,1)S(1)}, bf16[8,9,16,128]{3,2,1,0:T(8,128)(2,1)}, u32[]{:S(2)}) copy-start(bf16[8,9,16,128]{3,2,1,0:T(8,128)(2,1)} %copy-done.5) | copy-start | bytes 884740
  46.1 101.6 %copy-start.7 = (bf16[128,16,128]{2,1,0:T(8,128)(2,1)}, bf16[128,16,128]{2,1,0:T(8,128)(2,1)S(1)}, u32[]{:S(2)}) copy-start(bf16[128,16,128]{2,1,0:T(8,128)(2,1)S(1)} %pad_maximum_fusion.1.refs_7_) | copy-start | bytes 1572868
  46.1 21.6 %collective-permute-start.12 = (bf16[128,16,128]{2,1,0:T(8,128)(2,1)S(1)}, bf16[128,16,128]{2,1,0:T(8,128)(2,1)S(1)}, u32[]{:S(2)}, u32[]{:S(2)}) collective-permute-start(bf16[128,16,128]{2,1,0:T(8,128)(2,1)S(1)} %pad_maximum_fusion.1.refs_7_), channel_id=1, source_target_pairs={{0,2},{1,3},{2,4},{3,5},{4,6},{5,7},{6,8},{7,9},{8,10},{9,11},{10,... | collective-permute-start | bytes 1572872 | tf_op jit(solution)/shard_map/ppermute | solution.py:435
  50.1 19.5 %collective-permute-start.16 = (bf16[128,16,128]{2,1,0:T(8,128)(2,1)S(1)}, bf16[128,16,128]{2,1,0:T(8,128)(2,1)S(1)}, u32[]{:S(2)}, u32[]{:S(2)}) collective-permute-start(bf16[128,16,128]{2,1,0:T(8,128)(2,1)S(1)} %pad_maximum_fusion.1.refs_7_), channel_id=1, source_target_pairs={{0,14},{1,15},{2,0},{3,1},{4,2},{5,3},{6,4},{7,5},{8,6},{9,7},{10,... | collective-permute-start | bytes 1572872 | tf_op jit(solution)/shard_map/ppermute | solution.py:437
  58.8 88.9 %copy-start.8 = (bf16[128,16,128]{2,1,0:T(8,128)(2,1)}, bf16[128,16,128]{2,1,0:T(8,128)(2,1)S(1)}, u32[]{:S(2)}) copy-start(bf16[128,16,128]{2,1,0:T(8,128)(2,1)S(1)} %pad_maximum_fusion.refs_0_) | copy-start | bytes 1572868
  58.8 20.1 %collective-permute-start.1 = (bf16[128,16,128]{2,1,0:T(8,128)(2,1)S(1)}, bf16[128,16,128]{2,1,0:T(8,128)(2,1)S(1)}, u32[]{:S(2)}, u32[]{:S(2)}) collective-permute-start(bf16[128,16,128]{2,1,0:T(8,128)(2,1)S(1)} %pad_maximum_fusion.refs_0_), channel_id=1, source_target_pairs={{0,2},{1,3},{2,4},{3,5},{4,6},{5,7},{6,8},{7,9},{8,10},{9,11},{10,... | collective-permute-start | bytes 1572872 | tf_op jit(solution)/shard_map/ppermute | solution.py:435
  60.7 20.1 %collective-permute-start.8 = (bf16[128,16,128]{2,1,0:T(8,128)(2,1)S(1)}, bf16[128,16,128]{2,1,0:T(8,128)(2,1)S(1)}, u32[]{:S(2)}, u32[]{:S(2)}) collective-permute-start(bf16[128,16,128]{2,1,0:T(8,128)(2,1)S(1)} %pad_maximum_fusion.refs_0_), channel_id=1, source_target_pairs={{0,14},{1,15},{2,0},{3,1},{4,2},{5,3},{6,4},{7,5},{8,6},{9,7},{10,... | collective-permute-start | bytes 1572872 | tf_op jit(solution)/shard_map/ppermute | solution.py:437
  67.6 41.6 %copy-start.13 = (bf16[128,16,128]{2,1,0:T(8,128)(2,1)}, bf16[128,16,128]{2,1,0:T(8,128)(2,1)S(1)}, u32[]{:S(2)}) copy-start(bf16[128,16,128]{2,1,0:T(8,128)(2,1)S(1)} %collective-permute-done.12.refs_8_) | copy-start | bytes 1572868
  67.7 22.5 %collective-permute-start.13 = (bf16[128,16,128]{2,1,0:T(8,128)(2,1)S(1)}, bf16[128,16,128]{2,1,0:T(8,128)(2,1)S(1)}, u32[]{:S(2)}, u32[]{:S(2)}) collective-permute-start(bf16[128,16,128]{2,1,0:T(8,128)(2,1)S(1)} %collective-permute-done.12.refs_8_), channel_id=1, source_target_pairs={{0,2},{1,3},{2,4},{3,5},{4,6},{5,7},{6,8},{7,9},{8,10},{9,11},{10,... | collective-permute-start | bytes 1572872 | tf_op jit(solution)/shard_map/ppermute | solution.py:435
  69.6 39.7 %copy-start.14 = (bf16[128,16,128]{2,1,0:T(8,128)(2,1)}, bf16[128,16,128]{2,1,0:T(8,128)(2,1)S(1)}, u32[]{:S(2)}) copy-start(bf16[128,16,128]{2,1,0:T(8,128)(2,1)S(1)} %collective-permute-done.16.refs_9_) | copy-start | bytes 1572868
  69.6 22.5 %collective-permute-start.17 = (bf16[128,16,128]{2,1,0:T(8,128)(2,1)S(1)}, bf16[128,16,128]{2,1,0:T(8,128)(2,1)S(1)}, u32[]{:S(2)}, u32[]{:S(2)}) collective-permute-start(bf16[128,16,128]{2,1,0:T(8,128)(2,1)S(1)} %collective-permute-done.16.refs_9_), channel_id=1, source_target_pairs={{0,14},{1,15},{2,0},{3,1},{4,2},{5,3},{6,4},{7,5},{8,6},{9,7},{10,... | collective-permute-start | bytes 1572872 | tf_op jit(solution)/shard_map/ppermute | solution.py:437
  78.9 22.4 %collective-permute-start.2 = (bf16[128,16,128]{2,1,0:T(8,128)(2,1)S(1)}, bf16[128,16,128]{2,1,0:T(8,128)(2,1)S(1)}, u32[]{:S(2)}, u32[]{:S(2)}) collective-permute-start(bf16[128,16,128]{2,1,0:T(8,128)(2,1)S(1)} %collective-permute-done.1.refs_1_), channel_id=1, source_target_pairs={{0,2},{1,3},{2,4},{3,5},{4,6},{5,7},{6,8},{7,9},{8,10},{9,11},{10,... | collective-permute-start | bytes 1572872 | tf_op jit(solution)/shard_map/ppermute | solution.py:435
  80.8 22.3 %collective-permute-start.9 = (bf16[128,16,128]{2,1,0:T(8,128)(2,1)S(1)}, bf16[128,16,128]{2,1,0:T(8,128)(2,1)S(1)}, u32[]{:S(2)}, u32[]{:S(2)}) collective-permute-start(bf16[128,16,128]{2,1,0:T(8,128)(2,1)S(1)} %collective-permute-done.8.refs_2_), channel_id=1, source_target_pairs={{0,14},{1,15},{2,0},{3,1},{4,2},{5,3},{6,4},{7,5},{8,6},{9,7},{10,... | collective-permute-start | bytes 1572872 | tf_op jit(solution)/shard_map/ppermute | solution.py:437
  90.1 37.6 %copy-start.17 = (bf16[128,16,128]{2,1,0:T(8,128)(2,1)}, bf16[128,16,128]{2,1,0:T(8,128)(2,1)S(1)}, u32[]{:S(2)}) copy-start(bf16[128,16,128]{2,1,0:T(8,128)(2,1)S(1)} %collective-permute-done.13.refs_10_) | copy-start | bytes 1572868
  90.1 28.2 %collective-permute-start.14 = (bf16[128,16,128]{2,1,0:T(8,128)(2,1)S(1)}, bf16[128,16,128]{2,1,0:T(8,128)(2,1)S(1)}, u32[]{:S(2)}, u32[]{:S(2)}) collective-permute-start(bf16[128,16,128]{2,1,0:T(8,128)(2,1)S(1)} %collective-permute-done.13.refs_10_), channel_id=1, source_target_pairs={{0,2},{1,3},{2,4},{3,5},{4,6},{5,7},{6,8},{7,9},{8,10},{9,11},{10,... | collective-permute-start | bytes 1572872 | tf_op jit(solution)/shard_map/ppermute | solution.py:435
  92.0 40.3 %copy-start.18 = (bf16[128,16,128]{2,1,0:T(8,128)(2,1)}, bf16[128,16,128]{2,1,0:T(8,128)(2,1)S(1)}, u32[]{:S(2)}) copy-start(bf16[128,16,128]{2,1,0:T(8,128)(2,1)S(1)} %collective-permute-done.17.refs_11_) | copy-start | bytes 1572868
  92.1 28.2 %collective-permute-start.18 = (bf16[128,16,128]{2,1,0:T(8,128)(2,1)S(1)}, bf16[128,16,128]{2,1,0:T(8,128)(2,1)S(1)}, u32[]{:S(2)}, u32[]{:S(2)}) collective-permute-start(bf16[128,16,128]{2,1,0:T(8,128)(2,1)S(1)} %collective-permute-done.17.refs_11_), channel_id=1, source_target_pairs={{0,14},{1,15},{2,0},{3,1},{4,2},{5,3},{6,4},{7,5},{8,6},{9,7},{10,... | collective-permute-start | bytes 1572872 | tf_op jit(solution)/shard_map/ppermute | solution.py:437
  101.3 31.1 %copy-start.19 = (bf16[128,16,128]{2,1,0:T(8,128)(2,1)}, bf16[128,16,128]{2,1,0:T(8,128)(2,1)S(1)}, u32[]{:S(2)}) copy-start(bf16[128,16,128]{2,1,0:T(8,128)(2,1)S(1)} %collective-permute-done.2.refs_3_) | copy-start | bytes 1572868
  101.3 23.7 %collective-permute-start.3 = (bf16[128,16,128]{2,1,0:T(8,128)(2,1)S(1)}, bf16[128,16,128]{2,1,0:T(8,128)(2,1)S(1)}, u32[]{:S(2)}, u32[]{:S(2)}) collective-permute-start(bf16[128,16,128]{2,1,0:T(8,128)(2,1)S(1)} %collective-permute-done.2.refs_3_), channel_id=1, source_target_pairs={{0,2},{1,3},{2,4},{3,5},{4,6},{5,7},{6,8},{7,9},{8,10},{9,11},{10,... | collective-permute-start | bytes 1572872 | tf_op jit(solution)/shard_map/ppermute | solution.py:435
  103.2 23.7 %collective-permute-start.10 = (bf16[128,16,128]{2,1,0:T(8,128)(2,1)S(1)}, bf16[128,16,128]{2,1,0:T(8,128)(2,1)S(1)}, u32[]{:S(2)}, u32[]{:S(2)}) collective-permute-start(bf16[128,16,128]{2,1,0:T(8,128)(2,1)S(1)} %collective-permute-done.9.refs_4_), channel_id=1, source_target_pairs={{0,14},{1,15},{2,0},{3,1},{4,2},{5,3},{6,4},{7,5},{8,6},{9,7},{10,... | collective-permute-start | bytes 1572872 | tf_op jit(solution)/shard_map/ppermute | solution.py:437
  112.1 35.6 %copy-start.4 = (s32[144]{0:T(256)}, s32[144]{0:T(256)S(1)}, u32[]{:S(2)}) copy-start(s32[144]{0:T(256)S(1)} %plan_slots.1.plan_ref) | copy-start | bytes 1732
  112.1 12.8 %collective-permute-start.6 = (s32[144]{0:T(256)S(1)}, s32[144]{0:T(256)S(1)}, u32[]{:S(2)}, u32[]{:S(2)}) collective-permute-start(s32[144]{0:T(256)S(1)} %plan_slots.1.plan_ref), channel_id=1, source_target_pairs={{0,1},{1,0},{2,3},{3,2},{4,5},{5,4},{6,7},{7,6},{8,9},{9,8},{10,11... | collective-permute-start | bytes 1736 | tf_op jit(solution)/shard_map/ppermute | solution.py:442
  118.3 14.0 %collective-permute-start.15 = (bf16[64,16,128]{2,1,0:T(8,128)(2,1)S(1)}, bf16[64,16,128]{2,1,0:T(8,128)(2,1)S(1)}, u32[]{:S(2)}, u32[]{:S(2)}) collective-permute-start(bf16[64,16,128]{2,1,0:T(8,128)(2,1)S(1)} %slice.57), channel_id=1, source_target_pairs={{0,2},{1,3},{2,4},{3,5},{4,6},{5,7},{6,8},{7,9},{8,10},{9,11},{10,... | collective-permute-start | bytes 786440 | tf_op jit(solution)/shard_map/ppermute | solution.py:451
  120.3 12.0 %collective-permute-start.19 = (bf16[64,16,128]{2,1,0:T(8,128)(2,1)S(1)}, bf16[64,16,128]{2,1,0:T(8,128)(2,1)S(1)}, u32[]{:S(2)}, u32[]{:S(2)}) collective-permute-start(bf16[64,16,128]{2,1,0:T(8,128)(2,1)S(1)} %slice.58), channel_id=1, source_target_pairs={{0,14},{1,15},{2,0},{3,1},{4,2},{5,3},{6,4},{7,5},{8,6},{9,7},{10,... | collective-permute-start | bytes 786440 | tf_op jit(solution)/shard_map/ppermute | solution.py:452
  125.0 9.5 %collective-permute-start.7 = (bf16[64,16,128]{2,1,0:T(8,128)(2,1)S(1)}, bf16[64,16,128]{2,1,0:T(8,128)(2,1)S(1)}, u32[]{:S(2)}, u32[]{:S(2)}) collective-permute-start(bf16[64,16,128]{2,1,0:T(8,128)(2,1)S(1)} %slice.42), channel_id=1, source_target_pairs={{0,2},{1,3},{2,4},{3,5},{4,6},{5,7},{6,8},{7,9},{8,10},{9,11},{10,... | collective-permute-start | bytes 786440 | tf_op jit(solution)/shard_map/ppermute | solution.py:451
  127.7 7.9 %collective-permute-start.11 = (bf16[64,16,128]{2,1,0:T(8,128)(2,1)S(1)}, bf16[64,16,128]{2,1,0:T(8,128)(2,1)}, u32[]{:S(2)}, u32[]{:S(2)}) collective-permute-start(bf16[64,16,128]{2,1,0:T(8,128)(2,1)S(1)} %slice.54), channel_id=1, source_target_pairs={{0,14},{1,15},{2,0},{3,1},{4,2},{5,3},{6,4},{7,5},{8,6},{9,7},{10,... | collective-permute-start | bytes 786440 | tf_op jit(solution)/shard_map/ppermute | solution.py:452
  138.6 19.9 %collective-permute-start.20 = (bf16[128,128,128]{2,1,0:T(8,128)(2,1)}, bf16[128,128,128]{2,1,0:T(8,128)(2,1)}, u32[]{:S(2)}, u32[]{:S(2)}) collective-permute-start(bf16[128,128,128]{2,1,0:T(8,128)(2,1)} %all-to-all-done.1.arrived_hbm), channel_id=1, source_target_pairs={{0,1},{1,0},{2,3},{3,2},{4,5},{5,4},{6,7},{7,6},{8,9},{9,8},{10,11... | collective-permute-start | bytes 12582920 | tf_op jit(solution)/shard_map/ppermute | solution.py:456
  145.7 12.8 %collective-permute-start.21 = (bf16[64,128,128]{2,1,0:T(8,128)(2,1)}, bf16[64,128,128]{2,1,0:T(8,128)(2,1)}, u32[]{:S(2)}, u32[]{:S(2)}) collective-permute-start(bf16[64,128,128]{2,1,0:T(8,128)(2,1)} %bitcast.20), channel_id=1, source_target_pairs={{0,1},{1,0},{2,3},{3,2},{4,5},{5,4},{6,7},{7,6},{8,9},{9,8},{10,11... | collective-permute-start | bytes 6291464 | tf_op jit(solution)/shard_map/ppermute | solution.py:440
  (19 other events, 273.4 us)

commit v3 on v2

--- a/solution.py
+++ b/solution.py
@@ -192,20 +192,11 @@
     return jnp.dot(lefts, groups, preferred_element_type=jnp.float32)
 
 
-def own_kernel(places, plan_ref, other_plan_ref, arrived_hbm, left_hbm, *refs):
+def pick_kernel(places, own_plan_ref, other_plan_ref, *refs):
     piece_refs = refs[: len(places)]
-    (
-        sums_ref,
-        picked_hbm,
-        picked_ref,
-        wave_ref,
-        arrived_ref,
-        left_ref,
-        grouped_ref,
-        sems,
-        piece_sems,
-        picked_sems,
-    ) = refs[len(places) :]
+    own_hbm, other_hbm, own_ref, other_ref, wave_ref, piece_sems, own_sems, other_sems = refs[
+        len(places) :
+    ]
     op = lax.axis_index("op")
     copies = []
     for i, (base, step) in enumerate(places):
@@ -219,40 +210,74 @@
         )
     for copy in copies:
         copy.start()
+    for copy in copies:
+        copy.wait()
+    halves = (
+        (own_plan_ref, own_ref, own_hbm, own_sems),
+        (other_plan_ref, other_ref, other_hbm, other_sems),
+    )
+    for plan_ref, picked_ref, picked_hbm, sems in halves:
+
+        def pick(step, carry):
+            for i in range(UNROLL):
+                n = step * UNROLL + i
+                picked_ref[n] = wave_ref[(plan_ref[n] >> GROUP_BITS) & (2**SECTOR_BITS - 1)]
+            rows = pl.ds(step * UNROLL, UNROLL)
+            pltpu.make_async_copy(picked_ref.at[rows], picked_hbm.at[rows], sems.at[step]).start()
+            return carry
+
+        lax.fori_loop(0, plan_ref[PLAN - 1], pick, 0)
+    for plan_ref, picked_ref, picked_hbm, sems in halves:
+
+        def finish(step, carry):
+            rows = pl.ds(step * UNROLL, UNROLL)
+            pltpu.make_async_copy(picked_ref.at[rows], picked_hbm.at[rows], sems.at[step]).wait()
+            return carry
+
+        lax.fori_loop(0, plan_ref[PLAN - 1], finish, 0)
+
+
+def own_kernel(
+    plan_ref,
+    arrived_hbm,
+    left_hbm,
+    picked_hbm,
+    sums_ref,
+    arrived_ref,
+    left_ref,
+    grouped_ref,
+    sems,
+    picked_ref,
+    more_sems,
+):
+    steps = plan_ref[PLAN - 1]
 
     def picked_copy(step):
         rows = pl.ds(step * UNROLL, UNROLL)
-        return pltpu.make_async_copy(picked_ref.at[rows], picked_hbm.at[rows], picked_sems.at[step])
-
-    def pick(step, carry):
-        for i in range(UNROLL):
-            n = step * UNROLL + i
-            picked_ref[n] = wave_ref[(other_plan_ref[n] >> GROUP_BITS) & (2**SECTOR_BITS - 1)]
+        return pltpu.make_async_copy(picked_hbm.at[rows], picked_ref.at[rows], more_sems.at[step])
+
+    def start_step(step, carry):
         picked_copy(step).start()
         return carry
 
-    def finish_pick(step, carry):
+    def start_more():
+        lax.fori_loop(0, steps, start_step, 0)
+
+    def wait_step(step):
         picked_copy(step).wait()
-        return carry
-
-    other_steps = other_plan_ref[PLAN - 1]
-
-    def pieces_here():
-        for copy in copies:
-            copy.wait()
-        lax.fori_loop(0, other_steps, pick, 0)
 
     half_products(
         plan_ref,
         arrived_hbm,
         left_hbm,
-        lambda n, sector: wave_ref[sector],
+        lambda n, sector: picked_ref[n],
         arrived_ref,
         left_ref,
         grouped_ref,
         sems,
-        pieces_here,
-        lambda step: None,
+        lambda: None,
+        wait_step,
+        start_more,
     )
 
     def left(pair, carry):
@@ -261,7 +286,6 @@
         return carry
 
     lax.fori_loop(0, 4, left, 0)
-    lax.fori_loop(0, other_steps, finish_pick, 0)
 
 
 def other_kernel(
@@ -345,30 +369,45 @@
 COST = pl.CostEstimate(flops=2 * 128 * 128**3, bytes_accessed=16 * 2**20, transcendentals=0)
 
 
-def own_products(plan, other_plan, arrived, left, pieces):
+def pick_blocks(own_plan, other_plan, pieces):
+    width = pieces[0][0].shape[2]
+    count = len(pieces)
+    block = (PICKED, Z, 16, width)
+    return pl.pallas_call(
+        functools.partial(pick_kernel, [p[1:] for p in pieces]),
+        out_shape=(jax.ShapeDtypeStruct(block, jnp.bfloat16),) * 2,
+        in_specs=[SMEM, SMEM] + [HBM] * count,
+        out_specs=(HBM, HBM),
+        scratch_shapes=[
+            pltpu.VMEM(block, jnp.bfloat16),
+            pltpu.VMEM(block, jnp.bfloat16),
+            pltpu.VMEM((X * Y * 8, Z, 16, width), jnp.bfloat16),
+            pltpu.SemaphoreType.DMA((count,)),
+            pltpu.SemaphoreType.DMA((PICKED // UNROLL,)),
+            pltpu.SemaphoreType.DMA((PICKED // UNROLL,)),
+        ],
+        compiler_params=pltpu.CompilerParams(vmem_limit_bytes=60 * 2**20),
+        cost_estimate=COST,
+        name="pick_blocks",
+    )(own_plan, other_plan, *[p[0] for p in pieces])
+
+
+def own_products(plan, arrived, left, picked):
     width = arrived.shape[1]
-    count = len(pieces)
     return pl.pallas_call(
-        functools.partial(own_kernel, [p[1:] for p in pieces]),
-        out_shape=(
-            jax.ShapeDtypeStruct((8, width, width), jnp.float32),
-            jax.ShapeDtypeStruct((PICKED, Z, 16, width), jnp.bfloat16),
-        ),
-        in_specs=[SMEM, SMEM] + [HBM] * (2 + count),
-        out_specs=(VMEM, HBM),
-        scratch_shapes=[
-            pltpu.VMEM((PICKED, Z, 16, width), jnp.bfloat16),
-            pltpu.VMEM((X * Y * 8, Z, 16, width), jnp.bfloat16),
-        ]
-        + work_space(arrived, left)
+        own_kernel,
+        out_shape=jax.ShapeDtypeStruct((8, width, width), jnp.float32),
+        in_specs=[SMEM, HBM, HBM, HBM],
+        out_specs=VMEM,
+        scratch_shapes=work_space(arrived, left)
         + [
-            pltpu.SemaphoreType.DMA((count,)),
+            pltpu.VMEM(picked.shape, picked.dtype),
             pltpu.SemaphoreType.DMA((PICKED // UNROLL,)),
         ],
         compiler_params=pltpu.CompilerParams(vmem_limit_bytes=60 * 2**20),
         cost_estimate=COST,
         name="own_products",
-    )(plan, other_plan, arrived, left, *[p[0] for p in pieces])
+    )(plan, arrived, left, picked)
 
 
 def other_products(plan, arrived, left, picked, sums):
@@ -452,9 +491,10 @@
         last.append((ring_down(downs[n][-1][size:]), base + size, Z // 2))
     pieces += last
 
-    arrived, *_ = tie((arrived, *[p[0] for p in last]))
+    own_picked, picked = pick_blocks(own_plan, other_plan, pieces)
+    arrived, own_picked, picked = tie((arrived, own_picked, picked))
     other_arrived = swap(arrived)
-    sums, picked = own_products(own_plan, other_plan, arrived, own_left, pieces)
+    sums = own_products(own_plan, arrived, own_left, own_picked)
     partial_value = other_products(other_plan, other_arrived, other_left, picked, sums)
     got = lax.all_to_all(partial_value, "op", split_axis=0, concat_axis=0, tiled=True)
     return jnp.sum(got.reshape(Z, CORES, 8, 8, width).astype(jnp.float32), axis=0)

time: 190 us -> 185 us (0.974)
  Pallas kernels: 21.6 us -> 24.9 us
  starting transfers between devices: 92.5 us -> 89.5 us
  local copies, waits for them, and re-layouts: 7.96 us -> 5.68 us
    pallas_call x1 -> x2, Pallas kernels: 10.7 us -> 14.1 us  [the longest x1 7.52 us: own_products(): pl.pallas_call(own_kernel, out_shape=jax.ShapeDtypeStruct((8, width, widt...]
    all_to_all x1, waiting for transfers between devices: 2.96 us -> 0.01 us  [per_device(): lax.all_to_all(packed, 'sector', split_axis=0, concat_axis=0, tiled=True)]
    ppermute x1, starting transfers between devices: 7.15 us -> 5.1 us  [per_device(): other_arrived = swap(arrived)]
    unnamed x54 -> x52, local copies, waits for them, and re-layouts: 6.16 us -> 5.4 us
  transfers between devices with their start and end apart: 23 -> 23, of which waited for: 8 -> 8; matrix products, arithmetic and copies ran while one was open for 1% -> 0% of each run, Pallas kernels for 8% -> 10%
where the time goes in v3:
time: 185 us; the launch traced here: 184 us
  starting transfers between devices  89.5 us (48%)
  blocking collectives  39.1 us (21%)
  Pallas kernels  24.9 us (13%)
  waiting for transfers between devices  22.5 us (12%)
  local copies, waits for them, and re-layouts  5.68 us (3%)
    ppermute x6, starting transfers between devices, per_device(): chain.append(ring_down(chain[-1]))  31.5 us
    all_to_all x1, blocking collectives, per_device(): lax.all_to_all(partial_value, 'op', split_axis=0, concat_axis=0, tiled=True)  21.5 us
    ppermute x6, waiting for transfers between devices, per_device(): chain.append(ring_up(chain[-1]))  18.1 us
    all_to_all x1, blocking collectives, spread_column(): lax.all_to_all(jnp.broadcast_to(load, (Y,) + load.shape[1:]), 'sector', s...  17.6 us
    ppermute x6, starting transfers between devices, per_device(): chain.append(ring_up(chain[-1]))  13.6 us
    ppermute x3, starting transfers between devices, per_device(): lax.ppermute(column, 'sector', x_shift(d))  10.6 us
    ppermute x2, starting transfers between devices, per_device(): last.append((ring_down(downs[n][-1][size:]), base + size, Z // 2))  9.41 us
    all_to_all x1, starting transfers between devices, per_device(): lax.all_to_all(packed, 'sector', split_axis=0, concat_axis=0, tiled=True)  8.33 us
  transfers between devices with their start and end apart: 23, of which 8 were waited for; matrix products, arithmetic and copies ran while one was open for 0% of the time, Pallas kernels for 10%

profile of v3, /device:TPU:1, one launch (start us, length us, event | category | flops | bytes accessed | tf_op | source)
XLA Modules:
  0.0 184.0 jit_solution(6499969728592822709)
XLA Ops:
  1.1 17.6 %all_to_all.15 = bf16[8,9,16,128]{3,2,1,0:T(8,128)(2,1)S(1)} all-to-all(bf16[8,9,16,128]{3,2,1,0:T(8,128)(2,1)S(1)} %broadcast_in_dim.12), channel_id=1, replica_groups={{0,16,32,48,64,80,96,112},{128,144,160,176,192,208,224,240},{256,272,28..., dimensions={0} | all-to-all | bytes 589824 | tf_op jit(solution)/shard_map/all_to_all | solution.py:441
  18.8 5.3 %collective-permute-start.4 = (bf16[8,9,16,128]{3,2,0,1:T(8,128)(2,1)S(1)}, bf16[8,9,16,128]{3,2,0,1:T(8,128)(2,1)S(1)}, u32[]{:S(2)}, u32[]{:S(2)}) collective-permute-start(bf16[8,9,16,128]{3,2,0,1:T(8,128)(2,1)S(1)} %copy.9), channel_id=1, source_target_pairs={{0,256},{16,272},{32,288},{48,304},{64,320},{80,336},{96,352},{112... | collective-permute-start | bytes 884744 | tf_op jit(solution)/shard_map/ppermute | solution.py:461
  24.1 2.8 %collective-permute-start.5 = (bf16[8,9,16,128]{3,2,0,1:T(8,128)(2,1)S(1)}, bf16[8,9,16,128]{3,2,0,1:T(8,128)(2,1)S(1)}, u32[]{:S(2)}, u32[]{:S(2)}) collective-permute-start(bf16[8,9,16,128]{3,2,0,1:T(8,128)(2,1)S(1)} %copy.9), channel_id=1, source_target_pairs={{0,384},{16,400},{32,416},{48,432},{64,448},{80,464},{96,480},{112... | collective-permute-start | bytes 884744 | tf_op jit(solution)/shard_map/ppermute | solution.py:461
  26.9 2.5 %collective-permute-start = (bf16[8,9,16,128]{3,2,0,1:T(8,128)(2,1)S(1)}, bf16[8,9,16,128]{3,2,0,1:T(8,128)(2,1)S(1)}, u32[]{:S(2)}, u32[]{:S(2)}) collective-permute-start(bf16[8,9,16,128]{3,2,0,1:T(8,128)(2,1)S(1)} %copy.9), channel_id=1, source_target_pairs={{0,128},{16,144},{32,160},{48,176},{64,192},{80,208},{96,224},{112... | collective-permute-start | bytes 884744 | tf_op jit(solution)/shard_map/ppermute | solution.py:461
  32.8 2.0 %copy-done.1 = bf16[128,128,128]{2,1,0:T(8,128)(2,1)} copy-done((bf16[128,128,128]{2,1,0:T(8,128)(2,1)}, bf16[128,128,128]{2,1,0:T(8,128)(2,1)S(1)}, u32[]{:S(2)}) %copy-start.1) | copy-done | bytes 4194328
  35.7 8.3 %all-to-all-start.1 = ((bf16[128,128,128]{2,1,0:T(8,128)(2,1)}), bf16[128,128,128]{2,1,0:T(8,128)(2,1)}, u32[]{:S(2)}, u32[]{:S(2)}) async-start(bf16[128,128,128]{2,1,0:T(8,128)(2,1)} %copy-done.1), calls=%async_computation.1 | async-start | bytes 8388608 | tf_op jit(solution)/shard_map/all_to_all | solution.py:463
  44.2 4.0 %collective-permute-start.10 = (bf16[128,16,128]{2,1,0:T(8,128)(2,1)S(1)}, bf16[128,16,128]{2,1,0:T(8,128)(2,1)S(1)}, u32[]{:S(2)}, u32[]{:S(2)}) collective-permute-start(bf16[128,16,128]{2,1,0:T(8,128)(2,1)S(1)} %pad_maximum_fusion.1.refs_7_), channel_id=1, source_target_pairs={{0,2},{1,3},{2,4},{3,5},{4,6},{5,7},{6,8},{7,9},{8,10},{9,11},{10,... | collective-permute-start | bytes 1572872 | tf_op jit(solution)/shard_map/ppermute | solution.py:474
  48.2 8.6 %collective-permute-start.11 = (bf16[128,16,128]{2,1,0:T(8,128)(2,1)S(1)}, bf16[128,16,128]{2,1,0:T(8,128)(2,1)S(1)}, u32[]{:S(2)}, u32[]{:S(2)}) collective-permute-start(bf16[128,16,128]{2,1,0:T(8,128)(2,1)S(1)} %pad_maximum_fusion.1.refs_7_), channel_id=1, source_target_pairs={{0,14},{1,15},{2,0},{3,1},{4,2},{5,3},{6,4},{7,5},{8,6},{9,7},{10,... | collective-permute-start | bytes 1572872 | tf_op jit(solution)/shard_map/ppermute | solution.py:476
  56.9 1.9 %collective-permute-start.1 = (bf16[128,16,128]{2,1,0:T(8,128)(2,1)S(1)}, bf16[128,16,128]{2,1,0:T(8,128)(2,1)S(1)}, u32[]{:S(2)}, u32[]{:S(2)}) collective-permute-start(bf16[128,16,128]{2,1,0:T(8,128)(2,1)S(1)} %pad_maximum_fusion.refs_0_), channel_id=1, source_target_pairs={{0,2},{1,3},{2,4},{3,5},{4,6},{5,7},{6,8},{7,9},{8,10},{9,11},{10,... | collective-permute-start | bytes 1572872 | tf_op jit(solution)/shard_map/ppermute | solution.py:474
  58.9 4.6 %collective-permute-start.7 = (bf16[128,16,128]{2,1,0:T(8,128)(2,1)S(1)}, bf16[128,16,128]{2,1,0:T(8,128)(2,1)S(1)}, u32[]{:S(2)}, u32[]{:S(2)}) collective-permute-start(bf16[128,16,128]{2,1,0:T(8,128)(2,1)S(1)} %pad_maximum_fusion.refs_0_), channel_id=1, source_target_pairs={{0,14},{1,15},{2,0},{3,1},{4,2},{5,3},{6,4},{7,5},{8,6},{9,7},{10,... | collective-permute-start | bytes 1572872 | tf_op jit(solution)/shard_map/ppermute | solution.py:476
  63.4 2.8 %collective-permute-done.10.refs_8_ = bf16[128,16,128]{2,1,0:T(8,128)(2,1)S(1)} collective-permute-done((bf16[128,16,128]{2,1,0:T(8,128)(2,1)S(1)}, bf16[128,16,128]{2,1,0:T(8,128)(2,1)S(1)}, u32[]{:S(2)}, u32[]{:S(2)}) %collective-permute-start.10) | collective-permute-done | bytes 524320 | tf_op jit(solution)/shard_map/ppermute | solution.py:474
  66.2 1.9 %collective-permute-start.12 = (bf16[128,16,128]{2,1,0:T(8,128)(2,1)S(1)}, bf16[128,16,128]{2,1,0:T(8,128)(2,1)S(1)}, u32[]{:S(2)}, u32[]{:S(2)}) collective-permute-start(bf16[128,16,128]{2,1,0:T(8,128)(2,1)S(1)} %collective-permute-done.10.refs_8_), channel_id=1, source_target_pairs={{0,2},{1,3},{2,4},{3,5},{4,6},{5,7},{6,8},{7,9},{8,10},{9,11},{10,... | collective-permute-start | bytes 1572872 | tf_op jit(solution)/shard_map/ppermute | solution.py:474
  68.1 4.6 %collective-permute-start.13 = (bf16[128,16,128]{2,1,0:T(8,128)(2,1)S(1)}, bf16[128,16,128]{2,1,0:T(8,128)(2,1)S(1)}, u32[]{:S(2)}, u32[]{:S(2)}) collective-permute-start(bf16[128,16,128]{2,1,0:T(8,128)(2,1)S(1)} %collective-permute-done.11.refs_9_), channel_id=1, source_target_pairs={{0,14},{1,15},{2,0},{3,1},{4,2},{5,3},{6,4},{7,5},{8,6},{9,7},{10,... | collective-permute-start | bytes 1572872 | tf_op jit(solution)/shard_map/ppermute | solution.py:476
  72.7 4.7 %collective-permute-done.1.refs_1_ = bf16[128,16,128]{2,1,0:T(8,128)(2,1)S(1)} collective-permute-done((bf16[128,16,128]{2,1,0:T(8,128)(2,1)S(1)}, bf16[128,16,128]{2,1,0:T(8,128)(2,1)S(1)}, u32[]{:S(2)}, u32[]{:S(2)}) %collective-permute-start.1) | collective-permute-done | bytes 524320 | tf_op jit(solution)/shard_map/ppermute | solution.py:474
  79.4 4.6 %collective-permute-start.8 = (bf16[128,16,128]{2,1,0:T(8,128)(2,1)S(1)}, bf16[128,16,128]{2,1,0:T(8,128)(2,1)S(1)}, u32[]{:S(2)}, u32[]{:S(2)}) collective-permute-start(bf16[128,16,128]{2,1,0:T(8,128)(2,1)S(1)} %collective-permute-done.7.refs_2_), channel_id=1, source_target_pairs={{0,14},{1,15},{2,0},{3,1},{4,2},{5,3},{6,4},{7,5},{8,6},{9,7},{10,... | collective-permute-start | bytes 1572872 | tf_op jit(solution)/shard_map/ppermute | solution.py:476
  84.0 4.7 %collective-permute-done.12.refs_10_ = bf16[128,16,128]{2,1,0:T(8,128)(2,1)S(1)} collective-permute-done((bf16[128,16,128]{2,1,0:T(8,128)(2,1)S(1)}, bf16[128,16,128]{2,1,0:T(8,128)(2,1)S(1)}, u32[]{:S(2)}, u32[]{:S(2)}) %collective-permute-start.12) | collective-permute-done | bytes 524320 | tf_op jit(solution)/shard_map/ppermute | solution.py:474
  90.6 4.6 %collective-permute-start.15 = (bf16[128,16,128]{2,1,0:T(8,128)(2,1)S(1)}, bf16[128,16,128]{2,1,0:T(8,128)(2,1)S(1)}, u32[]{:S(2)}, u32[]{:S(2)}) collective-permute-start(bf16[128,16,128]{2,1,0:T(8,128)(2,1)S(1)} %collective-permute-done.13.refs_11_), channel_id=1, source_target_pairs={{0,14},{1,15},{2,0},{3,1},{4,2},{5,3},{6,4},{7,5},{8,6},{9,7},{10,... | collective-permute-start | bytes 1572872 | tf_op jit(solution)/shard_map/ppermute | solution.py:476
  95.2 4.7 %collective-permute-done.2.refs_3_ = bf16[128,16,128]{2,1,0:T(8,128)(2,1)S(1)} collective-permute-done((bf16[128,16,128]{2,1,0:T(8,128)(2,1)S(1)}, bf16[128,16,128]{2,1,0:T(8,128)(2,1)S(1)}, u32[]{:S(2)}, u32[]{:S(2)}) %collective-permute-start.2) | collective-permute-done | bytes 524320 | tf_op jit(solution)/shard_map/ppermute | solution.py:474
  101.8 4.6 %collective-permute-start.9 = (bf16[128,16,128]{2,1,0:T(8,128)(2,1)S(1)}, bf16[128,16,128]{2,1,0:T(8,128)(2,1)S(1)}, u32[]{:S(2)}, u32[]{:S(2)}) collective-permute-start(bf16[128,16,128]{2,1,0:T(8,128)(2,1)S(1)} %collective-permute-done.8.refs_4_), channel_id=1, source_target_pairs={{0,14},{1,15},{2,0},{3,1},{4,2},{5,3},{6,4},{7,5},{8,6},{9,7},{10,... | collective-permute-start | bytes 1572872 | tf_op jit(solution)/shard_map/ppermute | solution.py:476
  106.5 2.8 %plan_slots.1.own_plan_ref.plan_ref = s32[144]{0:T(256)S(1)} custom-call(bf16[8,16,128]{2,1,0:T(8,128)(2,1)S(1)} %slice_bitcast_fusion.3.refs_0_, bf16[8,16,128]{2,1,0:T(8,128)(2,1)S(1)} %slice_bitcast_fusion.2.refs_1_, bf16[8,16,128]{2,1,0:T(8,128)(2,1)S(1)} %slice_bitcast_fusion.1.refs_2_, bf16[8,16,128]{2,1,0:T(8,128)(2,1)S(1)} %slice_bitcast_fusion.refs_3_), custom_call_target="tpu_custom_call" | custom-call | tf_op jit(solution)/shard_map/plan_slots/pallas_call | solution.py:127
  109.3 5.3 %collective-permute-start.6 = (s32[144]{0:T(256)S(1)}, s32[144]{0:T(256)S(1)}, u32[]{:S(2)}, u32[]{:S(2)}) collective-permute-start(s32[144]{0:T(256)S(1)} %plan_slots.1.own_plan_ref.plan_ref), channel_id=1, source_target_pairs={{0,1},{1,0},{2,3},{3,2},{4,5},{5,4},{6,7},{7,6},{8,9},{9,8},{10,11... | collective-permute-start | bytes 1736 | tf_op jit(solution)/shard_map/ppermute | solution.py:481
  114.6 1.9 %collective-permute-start.18 = (bf16[64,16,128]{2,1,0:T(8,128)(2,1)S(1)}, bf16[64,16,128]{2,1,0:T(8,128)(2,1)S(1)}, u32[]{:S(2)}, u32[]{:S(2)}) collective-permute-start(bf16[64,16,128]{2,1,0:T(8,128)(2,1)S(1)} %slice.57), channel_id=1, source_target_pairs={{0,2},{1,3},{2,4},{3,5},{4,6},{5,7},{6,8},{7,9},{8,10},{9,11},{10,... | collective-permute-start | bytes 786440 | tf_op jit(solution)/shard_map/ppermute | solution.py:490
  116.6 4.6 %collective-permute-start.19 = (bf16[64,16,128]{2,1,0:T(8,128)(2,1)S(1)}, bf16[64,16,128]{2,1,0:T(8,128)(2,1)S(1)}, u32[]{:S(2)}, u32[]{:S(2)}) collective-permute-start(bf16[64,16,128]{2,1,0:T(8,128)(2,1)S(1)} %slice.58), channel_id=1, source_target_pairs={{0,14},{1,15},{2,0},{3,1},{4,2},{5,3},{6,4},{7,5},{8,6},{9,7},{10,... | collective-permute-start | bytes 786440 | tf_op jit(solution)/shard_map/ppermute | solution.py:491
  122.4 1.9 %collective-permute-start.16 = (bf16[64,16,128]{2,1,0:T(8,128)(2,1)S(1)}, bf16[64,16,128]{2,1,0:T(8,128)(2,1)S(1)}, u32[]{:S(2)}, u32[]{:S(2)}) collective-permute-start(bf16[64,16,128]{2,1,0:T(8,128)(2,1)S(1)} %slice.44), channel_id=1, source_target_pairs={{0,2},{1,3},{2,4},{3,5},{4,6},{5,7},{6,8},{7,9},{8,10},{9,11},{10,... | collective-permute-start | bytes 786440 | tf_op jit(solution)/shard_map/ppermute | solution.py:490
  124.4 4.8 %collective-permute-start.17 = (bf16[64,16,128]{2,1,0:T(8,128)(2,1)S(1)}, bf16[64,16,128]{2,1,0:T(8,128)(2,1)}, u32[]{:S(2)}, u32[]{:S(2)}) collective-permute-start(bf16[64,16,128]{2,1,0:T(8,128)(2,1)S(1)} %slice.56), channel_id=1, source_target_pairs={{0,14},{1,15},{2,0},{3,1},{4,2},{5,3},{6,4},{7,5},{8,6},{9,7},{10,... | collective-permute-start | bytes 786440 | tf_op jit(solution)/shard_map/ppermute | solution.py:491
  129.3 3.2 %collective-permute-done.16.refs_14_ = bf16[64,16,128]{2,1,0:T(8,128)(2,1)S(1)} collective-permute-done((bf16[64,16,128]{2,1,0:T(8,128)(2,1)S(1)}, bf16[64,16,128]{2,1,0:T(8,128)(2,1)S(1)}, u32[]{:S(2)}, u32[]{:S(2)}) %collective-permute-start.16) | collective-permute-done | bytes 262176 | tf_op jit(solution)/shard_map/ppermute | solution.py:490
  133.3 6.6 %pick_blocks.1 = (bf16[128,8,16,128]{3,2,1,0:T(8,128)(2,1)}, bf16[128,8,16,128]{3,2,1,0:T(8,128)(2,1)}) custom-call(s32[144]{0:T(256)} %copy-done.4, s32[144]{0:T(256)} %copy-done.25, bf16[128,16,128]{2,1,0:T(8,128)(2,1)} %copy-done.8, bf16[128,16,128]{2,1,0:T(8,128)(2,1)} %copy-done.16, bf16[128,16,128]{2,1,0:T(8,128)(2,1)} %copy-done.17, ...), custom_call_target="tpu_custom_call" | custom-call | flops 536870912 | bytes 16777216 | tf_op jit(solution)/shard_map/pick_blocks/pallas_call | solution.py:376
  139.8 5.1 %collective-permute-start.20 = (bf16[128,128,128]{2,1,0:T(8,128)(2,1)}, bf16[128,128,128]{2,1,0:T(8,128)(2,1)}, u32[]{:S(2)}, u32[]{:S(2)}) collective-permute-start(bf16[128,128,128]{2,1,0:T(8,128)(2,1)} %all-to-all-done.1.arrived_hbm), channel_id=1, source_target_pairs={{0,1},{1,0},{2,3},{3,2},{4,5},{5,4},{6,7},{7,6},{8,9},{9,8},{10,11... | collective-permute-start | bytes 12582920 | tf_op jit(solution)/shard_map/ppermute | solution.py:496
  145.0 1.9 %collective-permute-start.21 = (bf16[64,128,128]{2,1,0:T(8,128)(2,1)S(1)}, bf16[64,128,128]{2,1,0:T(8,128)(2,1)}, u32[]{:S(2)}, u32[]{:S(2)}) collective-permute-start(bf16[64,128,128]{2,1,0:T(8,128)(2,1)S(1)} %bitcast.21), channel_id=1, source_target_pairs={{0,1},{1,0},{2,3},{3,2},{4,5},{5,4},{6,7},{7,6},{8,9},{9,8},{10,11... | collective-permute-start | bytes 6291464 | tf_op jit(solution)/shard_map/ppermute | solution.py:479
  146.9 7.5 %own_products.1.sums_hbm = f32[8,128,128]{2,1,0:T(8,128)} custom-call(s32[144]{0:T(256)} %copy-done.4, bf16[128,128,128]{2,1,0:T(8,128)(2,1)} %all-to-all-done.1.arrived_hbm, bf16[64,128,128]{2,1,0:T(8,128)(2,1)} %bitcast.20, bf16[128,8,16,128]{3,2,1,0:T(8,128)(2,1)} %get-tuple-element.24.picked_hbm), custom_call_target="tpu_custom_call" | custom-call | flops 536870912 | bytes 16777216 | tf_op jit(solution)/shard_map/own_products/pallas_call | solution.py:397
  154.8 6.9 %other_products.1 = bf16[16,64,128]{2,1,0:T(8,128)(2,1)} custom-call(s32[144]{0:T(256)} %copy-done.25, bf16[128,128,128]{2,1,0:T(8,128)(2,1)} %collective-permute-done.20.arrived_hbm, bf16[64,128,128]{2,1,0:T(8,128)(2,1)} %collective-permute-done.21.left_hbm, bf16[128,8,16,128]{3,2,1,0:T(8,128)(2,1)} %get-tuple-element.23.picked_hbm, ...), custom_call_target="tpu_custom_call" | custom-call | flops 536870912 | bytes 16777216 | tf_op jit(solution)/shard_map/other_products/pallas_call | solution.py:415
  161.8 21.5 %all_to_all.16 = bf16[16,64,128]{2,1,0:T(8,128)(2,1)S(1)} all-to-all(bf16[16,64,128]{2,1,0:T(8,128)(2,1)} %other_products.1), channel_id=1, replica_groups=mesh['sector'=32,'op'=16] {'op'}, dimensions={0} | all-to-all | bytes 524288 | tf_op jit(solution)/shard_map/all_to_all | solution.py:499
  (98 shorter events, 14.5 us)
Async XLA Ops:
  18.8 16.1 %collective-permute-start.4 = (bf16[8,9,16,128]{3,2,0,1:T(8,128)(2,1)S(1)}, bf16[8,9,16,128]{3,2,0,1:T(8,128)(2,1)S(1)}, u32[]{:S(2)}, u32[]{:S(2)}) collective-permute-start(bf16[8,9,16,128]{3,2,0,1:T(8,128)(2,1)S(1)} %copy.9), channel_id=1, source_target_pairs={{0,256},{16,272},{32,288},{48,304},{64,320},{80,336},{96,352},{112... | collective-permute-start | bytes 884744 | tf_op jit(solution)/shard_map/ppermute | solution.py:461
  24.1 11.5 %collective-permute-start.5 = (bf16[8,9,16,128]{3,2,0,1:T(8,128)(2,1)S(1)}, bf16[8,9,16,128]{3,2,0,1:T(8,128)(2,1)S(1)}, u32[]{:S(2)}, u32[]{:S(2)}) collective-permute-start(bf16[8,9,16,128]{3,2,0,1:T(8,128)(2,1)S(1)} %copy.9), channel_id=1, source_target_pairs={{0,384},{16,400},{32,416},{48,432},{64,448},{80,464},{96,480},{112... | collective-permute-start | bytes 884744 | tf_op jit(solution)/shard_map/ppermute | solution.py:461
  26.9 8.8 %collective-permute-start = (bf16[8,9,16,128]{3,2,0,1:T(8,128)(2,1)S(1)}, bf16[8,9,16,128]{3,2,0,1:T(8,128)(2,1)S(1)}, u32[]{:S(2)}, u32[]{:S(2)}) collective-permute-start(bf16[8,9,16,128]{3,2,0,1:T(8,128)(2,1)S(1)} %copy.9), channel_id=1, source_target_pairs={{0,128},{16,144},{32,160},{48,176},{64,192},{80,208},{96,224},{112... | collective-permute-start | bytes 884744 | tf_op jit(solution)/shard_map/ppermute | solution.py:461
  35.7 104.2 %all-to-all-start.1 = ((bf16[128,128,128]{2,1,0:T(8,128)(2,1)}), bf16[128,128,128]{2,1,0:T(8,128)(2,1)}, u32[]{:S(2)}, u32[]{:S(2)}) async-start(bf16[128,128,128]{2,1,0:T(8,128)(2,1)} %copy-done.1), calls=%async_computation.1 | async-start | bytes 8388608 | tf_op jit(solution)/shard_map/all_to_all | solution.py:463
  44.0 39.9 %copy-start.6 = (bf16[8,9,16,128]{3,2,1,0:T(8,128)(2,1)S(1)}, bf16[8,9,16,128]{3,2,1,0:T(8,128)(2,1)}, u32[]{:S(2)}) copy-start(bf16[8,9,16,128]{3,2,1,0:T(8,128)(2,1)} %copy-done.5) | copy-start | bytes 884740
  44.2 89.0 %copy-start.7 = (bf16[128,16,128]{2,1,0:T(8,128)(2,1)}, bf16[128,16,128]{2,1,0:T(8,128)(2,1)S(1)}, u32[]{:S(2)}) copy-start(bf16[128,16,128]{2,1,0:T(8,128)(2,1)S(1)} %pad_maximum_fusion.1.refs_7_) | copy-start | bytes 1572868
  44.2 22.0 %collective-permute-start.10 = (bf16[128,16,128]{2,1,0:T(8,128)(2,1)S(1)}, bf16[128,16,128]{2,1,0:T(8,128)(2,1)S(1)}, u32[]{:S(2)}, u32[]{:S(2)}) collective-permute-start(bf16[128,16,128]{2,1,0:T(8,128)(2,1)S(1)} %pad_maximum_fusion.1.refs_7_), channel_id=1, source_target_pairs={{0,2},{1,3},{2,4},{3,5},{4,6},{5,7},{6,8},{7,9},{8,10},{9,11},{10,... | collective-permute-start | bytes 1572872 | tf_op jit(solution)/shard_map/ppermute | solution.py:474
  48.2 19.9 %collective-permute-start.11 = (bf16[128,16,128]{2,1,0:T(8,128)(2,1)S(1)}, bf16[128,16,128]{2,1,0:T(8,128)(2,1)S(1)}, u32[]{:S(2)}, u32[]{:S(2)}) collective-permute-start(bf16[128,16,128]{2,1,0:T(8,128)(2,1)S(1)} %pad_maximum_fusion.1.refs_7_), channel_id=1, source_target_pairs={{0,14},{1,15},{2,0},{3,1},{4,2},{5,3},{6,4},{7,5},{8,6},{9,7},{10,... | collective-permute-start | bytes 1572872 | tf_op jit(solution)/shard_map/ppermute | solution.py:476
  56.9 76.3 %copy-start.8 = (bf16[128,16,128]{2,1,0:T(8,128)(2,1)}, bf16[128,16,128]{2,1,0:T(8,128)(2,1)S(1)}, u32[]{:S(2)}) copy-start(bf16[128,16,128]{2,1,0:T(8,128)(2,1)S(1)} %pad_maximum_fusion.refs_0_) | copy-start | bytes 1572868
  56.9 20.5 %collective-permute-start.1 = (bf16[128,16,128]{2,1,0:T(8,128)(2,1)S(1)}, bf16[128,16,128]{2,1,0:T(8,128)(2,1)S(1)}, u32[]{:S(2)}, u32[]{:S(2)}) collective-permute-start(bf16[128,16,128]{2,1,0:T(8,128)(2,1)S(1)} %pad_maximum_fusion.refs_0_), channel_id=1, source_target_pairs={{0,2},{1,3},{2,4},{3,5},{4,6},{5,7},{6,8},{7,9},{8,10},{9,11},{10,... | collective-permute-start | bytes 1572872 | tf_op jit(solution)/shard_map/ppermute | solution.py:474
  58.9 20.5 %collective-permute-start.7 = (bf16[128,16,128]{2,1,0:T(8,128)(2,1)S(1)}, bf16[128,16,128]{2,1,0:T(8,128)(2,1)S(1)}, u32[]{:S(2)}, u32[]{:S(2)}) collective-permute-start(bf16[128,16,128]{2,1,0:T(8,128)(2,1)S(1)} %pad_maximum_fusion.refs_0_), channel_id=1, source_target_pairs={{0,14},{1,15},{2,0},{3,1},{4,2},{5,3},{6,4},{7,5},{8,6},{9,7},{10,... | collective-permute-start | bytes 1572872 | tf_op jit(solution)/shard_map/ppermute | solution.py:476
  66.2 40.3 %copy-start.14 = (bf16[128,16,128]{2,1,0:T(8,128)(2,1)}, bf16[128,16,128]{2,1,0:T(8,128)(2,1)S(1)}, u32[]{:S(2)}) copy-start(bf16[128,16,128]{2,1,0:T(8,128)(2,1)S(1)} %collective-permute-done.10.refs_8_) | copy-start | bytes 1572868
  66.2 22.5 %collective-permute-start.12 = (bf16[128,16,128]{2,1,0:T(8,128)(2,1)S(1)}, bf16[128,16,128]{2,1,0:T(8,128)(2,1)S(1)}, u32[]{:S(2)}, u32[]{:S(2)}) collective-permute-start(bf16[128,16,128]{2,1,0:T(8,128)(2,1)S(1)} %collective-permute-done.10.refs_8_), channel_id=1, source_target_pairs={{0,2},{1,3},{2,4},{3,5},{4,6},{5,7},{6,8},{7,9},{8,10},{9,11},{10,... | collective-permute-start | bytes 1572872 | tf_op jit(solution)/shard_map/ppermute | solution.py:474
  68.1 38.3 %copy-start.15 = (bf16[128,16,128]{2,1,0:T(8,128)(2,1)}, bf16[128,16,128]{2,1,0:T(8,128)(2,1)S(1)}, u32[]{:S(2)}) copy-start(bf16[128,16,128]{2,1,0:T(8,128)(2,1)S(1)} %collective-permute-done.11.refs_9_) | copy-start | bytes 1572868
  68.1 22.5 %collective-permute-start.13 = (bf16[128,16,128]{2,1,0:T(8,128)(2,1)S(1)}, bf16[128,16,128]{2,1,0:T(8,128)(2,1)S(1)}, u32[]{:S(2)}, u32[]{:S(2)}) collective-permute-start(bf16[128,16,128]{2,1,0:T(8,128)(2,1)S(1)} %collective-permute-done.11.refs_9_), channel_id=1, source_target_pairs={{0,14},{1,15},{2,0},{3,1},{4,2},{5,3},{6,4},{7,5},{8,6},{9,7},{10,... | collective-permute-start | bytes 1572872 | tf_op jit(solution)/shard_map/ppermute | solution.py:476
  77.4 22.5 %collective-permute-start.2 = (bf16[128,16,128]{2,1,0:T(8,128)(2,1)S(1)}, bf16[128,16,128]{2,1,0:T(8,128)(2,1)S(1)}, u32[]{:S(2)}, u32[]{:S(2)}) collective-permute-start(bf16[128,16,128]{2,1,0:T(8,128)(2,1)S(1)} %collective-permute-done.1.refs_1_), channel_id=1, source_target_pairs={{0,2},{1,3},{2,4},{3,5},{4,6},{5,7},{6,8},{7,9},{8,10},{9,11},{10,... | collective-permute-start | bytes 1572872 | tf_op jit(solution)/shard_map/ppermute | solution.py:474
  79.4 22.5 %collective-permute-start.8 = (bf16[128,16,128]{2,1,0:T(8,128)(2,1)S(1)}, bf16[128,16,128]{2,1,0:T(8,128)(2,1)S(1)}, u32[]{:S(2)}, u32[]{:S(2)}) collective-permute-start(bf16[128,16,128]{2,1,0:T(8,128)(2,1)S(1)} %collective-permute-done.7.refs_2_), channel_id=1, source_target_pairs={{0,14},{1,15},{2,0},{3,1},{4,2},{5,3},{6,4},{7,5},{8,6},{9,7},{10,... | collective-permute-start | bytes 1572872 | tf_op jit(solution)/shard_map/ppermute | solution.py:476
  88.7 40.6 %copy-start.18 = (bf16[128,16,128]{2,1,0:T(8,128)(2,1)}, bf16[128,16,128]{2,1,0:T(8,128)(2,1)S(1)}, u32[]{:S(2)}) copy-start(bf16[128,16,128]{2,1,0:T(8,128)(2,1)S(1)} %collective-permute-done.12.refs_10_) | copy-start | bytes 1572868
  88.7 25.9 %collective-permute-start.14 = (bf16[128,16,128]{2,1,0:T(8,128)(2,1)S(1)}, bf16[128,16,128]{2,1,0:T(8,128)(2,1)S(1)}, u32[]{:S(2)}, u32[]{:S(2)}) collective-permute-start(bf16[128,16,128]{2,1,0:T(8,128)(2,1)S(1)} %collective-permute-done.12.refs_10_), channel_id=1, source_target_pairs={{0,2},{1,3},{2,4},{3,5},{4,6},{5,7},{6,8},{7,9},{8,10},{9,11},{10,... | collective-permute-start | bytes 1572872 | tf_op jit(solution)/shard_map/ppermute | solution.py:474
  90.6 41.9 %copy-start.19 = (bf16[128,16,128]{2,1,0:T(8,128)(2,1)}, bf16[128,16,128]{2,1,0:T(8,128)(2,1)S(1)}, u32[]{:S(2)}) copy-start(bf16[128,16,128]{2,1,0:T(8,128)(2,1)S(1)} %collective-permute-done.13.refs_11_) | copy-start | bytes 1572868
  90.6 25.9 %collective-permute-start.15 = (bf16[128,16,128]{2,1,0:T(8,128)(2,1)S(1)}, bf16[128,16,128]{2,1,0:T(8,128)(2,1)S(1)}, u32[]{:S(2)}, u32[]{:S(2)}) collective-permute-start(bf16[128,16,128]{2,1,0:T(8,128)(2,1)S(1)} %collective-permute-done.13.refs_11_), channel_id=1, source_target_pairs={{0,14},{1,15},{2,0},{3,1},{4,2},{5,3},{6,4},{7,5},{8,6},{9,7},{10,... | collective-permute-start | bytes 1572872 | tf_op jit(solution)/shard_map/ppermute | solution.py:476
  99.9 32.6 %copy-start.20 = (bf16[128,16,128]{2,1,0:T(8,128)(2,1)}, bf16[128,16,128]{2,1,0:T(8,128)(2,1)S(1)}, u32[]{:S(2)}) copy-start(bf16[128,16,128]{2,1,0:T(8,128)(2,1)S(1)} %collective-permute-done.2.refs_3_) | copy-start | bytes 1572868
  99.9 22.5 %collective-permute-start.3 = (bf16[128,16,128]{2,1,0:T(8,128)(2,1)S(1)}, bf16[128,16,128]{2,1,0:T(8,128)(2,1)S(1)}, u32[]{:S(2)}, u32[]{:S(2)}) collective-permute-start(bf16[128,16,128]{2,1,0:T(8,128)(2,1)S(1)} %collective-permute-done.2.refs_3_), channel_id=1, source_target_pairs={{0,2},{1,3},{2,4},{3,5},{4,6},{5,7},{6,8},{7,9},{8,10},{9,11},{10,... | collective-permute-start | bytes 1572872 | tf_op jit(solution)/shard_map/ppermute | solution.py:474
  101.8 30.6 %copy-start.21 = (bf16[128,16,128]{2,1,0:T(8,128)(2,1)}, bf16[128,16,128]{2,1,0:T(8,128)(2,1)S(1)}, u32[]{:S(2)}) copy-start(bf16[128,16,128]{2,1,0:T(8,128)(2,1)S(1)} %collective-permute-done.8.refs_4_) | copy-start | bytes 1572868
  101.8 22.5 %collective-permute-start.9 = (bf16[128,16,128]{2,1,0:T(8,128)(2,1)S(1)}, bf16[128,16,128]{2,1,0:T(8,128)(2,1)S(1)}, u32[]{:S(2)}, u32[]{:S(2)}) collective-permute-start(bf16[128,16,128]{2,1,0:T(8,128)(2,1)S(1)} %collective-permute-done.8.refs_4_), channel_id=1, source_target_pairs={{0,14},{1,15},{2,0},{3,1},{4,2},{5,3},{6,4},{7,5},{8,6},{9,7},{10,... | collective-permute-start | bytes 1572872 | tf_op jit(solution)/shard_map/ppermute | solution.py:476
  109.3 11.9 %collective-permute-start.6 = (s32[144]{0:T(256)S(1)}, s32[144]{0:T(256)S(1)}, u32[]{:S(2)}, u32[]{:S(2)}) collective-permute-start(s32[144]{0:T(256)S(1)} %plan_slots.1.own_plan_ref.plan_ref), channel_id=1, source_target_pairs={{0,1},{1,0},{2,3},{3,2},{4,5},{5,4},{6,7},{7,6},{8,9},{9,8},{10,11... | collective-permute-start | bytes 1736 | tf_op jit(solution)/shard_map/ppermute | solution.py:481
  114.6 14.7 %collective-permute-start.18 = (bf16[64,16,128]{2,1,0:T(8,128)(2,1)S(1)}, bf16[64,16,128]{2,1,0:T(8,128)(2,1)S(1)}, u32[]{:S(2)}, u32[]{:S(2)}) collective-permute-start(bf16[64,16,128]{2,1,0:T(8,128)(2,1)S(1)} %slice.57), channel_id=1, source_target_pairs={{0,2},{1,3},{2,4},{3,5},{4,6},{5,7},{6,8},{7,9},{8,10},{9,11},{10,... | collective-permute-start | bytes 786440 | tf_op jit(solution)/shard_map/ppermute | solution.py:490
  116.6 12.7 %collective-permute-start.19 = (bf16[64,16,128]{2,1,0:T(8,128)(2,1)S(1)}, bf16[64,16,128]{2,1,0:T(8,128)(2,1)S(1)}, u32[]{:S(2)}, u32[]{:S(2)}) collective-permute-start(bf16[64,16,128]{2,1,0:T(8,128)(2,1)S(1)} %slice.58), channel_id=1, source_target_pairs={{0,14},{1,15},{2,0},{3,1},{4,2},{5,3},{6,4},{7,5},{8,6},{9,7},{10,... | collective-permute-start | bytes 786440 | tf_op jit(solution)/shard_map/ppermute | solution.py:491
  122.4 10.1 %collective-permute-start.16 = (bf16[64,16,128]{2,1,0:T(8,128)(2,1)S(1)}, bf16[64,16,128]{2,1,0:T(8,128)(2,1)S(1)}, u32[]{:S(2)}, u32[]{:S(2)}) collective-permute-start(bf16[64,16,128]{2,1,0:T(8,128)(2,1)S(1)} %slice.44), channel_id=1, source_target_pairs={{0,2},{1,3},{2,4},{3,5},{4,6},{5,7},{6,8},{7,9},{8,10},{9,11},{10,... | collective-permute-start | bytes 786440 | tf_op jit(solution)/shard_map/ppermute | solution.py:490
  124.4 8.8 %collective-permute-start.17 = (bf16[64,16,128]{2,1,0:T(8,128)(2,1)S(1)}, bf16[64,16,128]{2,1,0:T(8,128)(2,1)}, u32[]{:S(2)}, u32[]{:S(2)}) collective-permute-start(bf16[64,16,128]{2,1,0:T(8,128)(2,1)S(1)} %slice.56), channel_id=1, source_target_pairs={{0,14},{1,15},{2,0},{3,1},{4,2},{5,3},{6,4},{7,5},{8,6},{9,7},{10,... | collective-permute-start | bytes 786440 | tf_op jit(solution)/shard_map/ppermute | solution.py:491
  139.8 15.0 %collective-permute-start.20 = (bf16[128,128,128]{2,1,0:T(8,128)(2,1)}, bf16[128,128,128]{2,1,0:T(8,128)(2,1)}, u32[]{:S(2)}, u32[]{:S(2)}) collective-permute-start(bf16[128,128,128]{2,1,0:T(8,128)(2,1)} %all-to-all-done.1.arrived_hbm), channel_id=1, source_target_pairs={{0,1},{1,0},{2,3},{3,2},{4,5},{5,4},{6,7},{7,6},{8,9},{9,8},{10,11... | collective-permute-start | bytes 12582920 | tf_op jit(solution)/shard_map/ppermute | solution.py:496
  145.0 9.9 %collective-permute-start.21 = (bf16[64,128,128]{2,1,0:T(8,128)(2,1)S(1)}, bf16[64,128,128]{2,1,0:T(8,128)(2,1)}, u32[]{:S(2)}, u32[]{:S(2)}) collective-permute-start(bf16[64,128,128]{2,1,0:T(8,128)(2,1)S(1)} %bitcast.21), channel_id=1, source_target_pairs={{0,1},{1,0},{2,3},{3,2},{4,5},{5,4},{6,7},{7,6},{8,9},{9,8},{10,11... | collective-permute-start | bytes 6291464 | tf_op jit(solution)/shard_map/ppermute | solution.py:479
  (18 other events, 193.6 us)
